TPU v7x, 32 devices: a whole 2x2x4 slice. The times are simulated.
32 devices in a mesh: grp: 4 (over y, x), tile: 8 (over z, core).
Axes of the slice: x: 2, y: 2, z: 4, core: 2. Of those that a mesh axis runs over, the one named last changes fastest.
Arguments:
- screens: bfloat16 [3, 32768, 256], P(None, ('grp', 'tile')), may hold values from -4 to 4
- interp_weights: bfloat16 [3, 4, 256, 256], replicated, may hold values from -0.375 to 0.375
- footprint: int32 [8192, 3, 4], P(('grp', 'tile')), may hold values from 0 to 32767, as said below
- illumination: float32 [8192, 256], P(('grp', 'tile')), may hold values from 0.3 to 1
- cm_values: bfloat16 [896, 16, 16, 2, 128], P('tile', 'grp'), may hold values from -0.09375 to 0.09375
- cm_columns: int32 [896, 16], P('tile', 'grp'), may hold values from 0 to 63, as said below
- prev_commands: float32 [14336], P('tile'), may hold values from 0 to 5
- owner_map: int32 [14336], P('tile'), may hold values from 0 to 2, as said below
- dm_gain: float32 [3], replicated, may hold values from 0.2 to 1
Outputs:
- slopes: float32 [2, 8192], P(None, ('grp', 'tile'))
- commands: float32 [14336], P('tile')
Inputs may be any that keep to these rules, and one draw needn't show every extreme that they name: `footprint`: the blocks of subaperture s lie among the 1024 blocks of the device holding s and the 256 blocks on either side of them, counted cyclically over all 32768 blocks; some subaperture reaches each end. `cm_columns`: nonzero block n names a column block from (n // 4) * 16 up to that plus 16 - 1. `owner_map`: every mirror owns some actuator.
All inputs are finite; a program needn't handle non-finite values.
Results may differ from a plain program's by a relative error of at most 0.0024.
Values may be sent and summed in bfloat16 or wider, within the bound.
A program may use at most 64 MiB of HBM per device.

v0:
```python
import math

import jax
import jax.numpy as jnp
from jax import lax
from jax.sharding import PartitionSpec as P

SIDE = 16


def from_behind(block, axis, distance):
    devices = range(lax.axis_size(axis))
    route = [((i - distance) % len(devices), i) for i in devices]
    return lax.ppermute(block, axis, route)


def spectrum_tables(side):
    pixels = side * side
    index = jnp.arange(pixels, dtype=jnp.int32)
    row_ids = index // side
    col_ids = index % side
    turns = (row_ids[:, None] * row_ids[None, :] + col_ids[:, None] * col_ids[None, :]) % side
    angle = turns.astype(jnp.float32) * (2.0 * math.pi / side)
    cosine = jnp.cos(angle)
    sine = jnp.sin(angle)
    table = jnp.concatenate(
        [jnp.concatenate([cosine, -sine], 1), jnp.concatenate([sine, cosine], 1)], 0
    )
    half = side // 2
    centre_v = (col_ids - side * (col_ids >= half).astype(jnp.int32)).astype(jnp.float32)
    centre_u = (row_ids - side * (row_ids >= half).astype(jnp.int32)).astype(jnp.float32)
    return (table.astype(jnp.bfloat16), centre_v, centre_u)


def mirror_update(recon, prev_part, owner_part, dm_gain):
    mirrors = dm_gain.shape[0]
    onehot = (owner_part[:, None] == jnp.arange(mirrors, dtype=jnp.int32)[None, :]).astype(
        jnp.float32
    )
    gains = jnp.sum(onehot * dm_gain[None, :], axis=1)
    updated = prev_part - gains * recon
    sums = jnp.sum(onehot * updated[:, None], axis=0)
    counts = jnp.sum(onehot, axis=0)
    return (onehot, updated, sums, counts)


def on_device(
    screens,
    interp_weights,
    footprint,
    illumination,
    cm_values,
    cm_columns,
    prev_commands,
    owner_map,
    dm_gain,
):
    layers, blk_dev, pixels = screens.shape
    sub_dev = footprint.shape[0]
    foot = footprint.shape[2]
    devices = lax.axis_size(("grp", "tile"))
    here = lax.axis_index(("grp", "tile"))
    reach = blk_dev // 4
    before = from_behind(screens[:, blk_dev - reach :, :], ("grp", "tile"), 1)
    after = from_behind(screens[:, :reach, :], ("grp", "tile"), -1)
    extended = jnp.concatenate([before, screens, after], axis=1)
    start = here * blk_dev - reach
    local_ids = jnp.mod(footprint - start, blk_dev * devices)
    picked = jnp.stack(
        [jnp.take(extended[layer], local_ids[:, layer, :], axis=0) for layer in range(layers)],
        axis=1,
    )
    picked = picked.reshape(sub_dev, layers * foot * pixels)
    weights_flat = interp_weights.reshape(layers * foot * pixels, pixels)
    phase = jnp.dot(picked, weights_flat, preferred_element_type=jnp.float32)
    side = SIDE
    table, centre_v, centre_u = spectrum_tables(side)
    field = jnp.concatenate(
        [illumination * jnp.cos(phase), illumination * jnp.sin(phase)], 1
    ).astype(jnp.bfloat16)
    spectrum = jnp.dot(field, table, preferred_element_type=jnp.float32)
    real_part = spectrum[:, :pixels]
    imag_part = spectrum[:, pixels:]
    intensity = real_part * real_part + imag_part * imag_part
    total = jnp.sum(intensity, axis=1)
    slope_x = jnp.sum(intensity * centre_v[None, :], axis=1) / total
    slope_y = jnp.sum(intensity * centre_u[None, :], axis=1) / total
    slopes = jnp.stack([slope_x, slope_y], 0)
    slope_words = slopes.astype(jnp.bfloat16)
    block_width = cm_values.shape[4]
    gathered = lax.all_gather(slope_words, "tile", axis=1, tiled=True)
    column_base = lax.axis_index("grp") * (gathered.shape[1] // block_width)
    blocks = gathered.reshape(2, gathered.shape[1] // block_width, block_width)
    chosen = jnp.take(blocks, cm_columns - column_base, axis=1)
    partial_value = jnp.einsum(
        "rjics,crjs->ri", cm_values, chosen, preferred_element_type=jnp.float32
    ).reshape(-1)
    recon = lax.psum(partial_value, "grp")
    onehot, updated, sums, counts = mirror_update(recon, prev_commands, owner_map, dm_gain)
    total_sums, total_counts = lax.psum((sums, counts), "tile")
    piston = total_sums / total_counts
    commands = updated - jnp.sum(onehot * piston[None, :], axis=1)
    return (slopes, commands)


def solution(mesh):
    in_specs = (
        P(None, ("grp", "tile"), None),
        P(),
        P(("grp", "tile"), None, None),
        P(("grp", "tile"), None),
        P("tile", "grp", None, None, None),
        P("tile", "grp"),
        P("tile"),
        P("tile"),
        P(),
    )
    out_specs = (P(None, ("grp", "tile")), P("tile"))
    return jax.shard_map(
        on_device, mesh=mesh, in_specs=in_specs, out_specs=out_specs, check_vma=False
    )
```

profile of v0, /device:TPU:0, one launch (start us, length us, event | category | flops | bytes accessed | tf_op | source)
XLA Modules:
  0.0 87.2 jit_solution(12775271344612463601)
XLA Ops:
  0.7 2.2 %fusion.44 = (bf16[3,256,256]{2,1,0:T(8,128)(2,1)}, bf16[3,256,256]{2,1,0:T(8,128)(2,1)}) fusion(bf16[3,1024,256]{2,1,0:T(8,128)(2,1)} %param.11), kind=kLoop, calls=%fused_computation.99 | loop fusion | bytes 1572864 | tf_op jit(solution)/shard_map/slice | solution.py:65
  2.9 0.5 collective-permute-start
  3.4 5.9 %collective-permute-start.1 = (bf16[3,256,256]{2,1,0:T(8,128)(2,1)}, bf16[3,256,256]{2,1,0:T(8,128)(2,1)}, u32[]{:S(2)}, u32[]{:S(2)}) collective-permute-start(bf16[3,256,256]{2,1,0:T(8,128)(2,1)} %get-tuple-element.17), channel_id=1, source_target_pairs={{1,0},{2,1},{3,2},{4,3},{5,4},{6,5},{7,6},{8,7},{9,8},{10,9},{11,1... | collective-permute-start | bytes 1179656 | tf_op jit(solution)/shard_map/ppermute | solution.py:14
  9.3 0.7 add_select_fusion.1
  10.0 0.6 compare_and_fusion.2
  11.4 1.9 %negate_convert_fusion = (bf16[256,256]{1,0:T(8,128)(2,1)S(1)}, bf16[256,256]{1,0:T(8,128)(2,1)}, bf16[256,256]{1,0:T(8,128)(2,1)}) fusion(s32[256]{0:T(256)S(1)} %get-tuple-element.32, s32[256]{0:T(256)S(1)} %get-tuple-element.33), kind=kLoop, calls=%fused_computation.46 | loop fusion | flops 1310720 | bytes 395264 | tf_op jit(solution)/shard_map/convert.5
  13.6 0.6 fusion.38
  14.2 1.8 %copy.33 = f32[256,256]{0,1:T(8,128)} copy(f32[256,256]{1,0:T(8,128)} %param.14) | data formatting | bytes 524288 | tf_op args[3]
  16.0 0.7 copy.35
  16.7 0.7 select_reduce_fusion.2
  17.4 1.0 %constant_dynamic-update-slice_fusion.2 = bf16[3,1536,256]{2,1,0:T(8,128)(2,1)S(1)} fusion(bf16[3,256,256]{2,1,0:T(8,128)(2,1)} %collective-permute-done), kind=kLoop, calls=%fused_computation.68 | loop fusion | bytes 786432
  18.5 1.0 %constant_dynamic-update-slice_fusion = bf16[3,1536,256]{2,1,0:T(8,128)(2,1)S(1)} fusion(bf16[3,1536,256]{2,1,0:T(8,128)(2,1)S(1)} %constant_dynamic-update-slice_fusion.1, bf16[3,256,256]{2,1,0:T(8,128)(2,1)} %collective-permute-done.1), kind=kLoop, calls=%fused_computation.66 | loop fusion | bytes 786432 | tf_op jit(solution)/shard_map/concatenate | solution.py:66
  19.6 1.0 %slice_bitcast_fusion.2 = (bf16[1536,256]{1,0:T(8,128)(2,1)S(1)}, bf16[1536,256]{1,0:T(8,128)(2,1)S(1)}, bf16[1536,256]{1,0:T(8,128)(2,1)}) fusion(bf16[3,1536,256]{2,1,0:T(8,128)(2,1)S(1)} %constant_dynamic-update-slice_fusion), kind=kLoop, calls=%fused_computation.15 | loop fusion | bytes 4718592 | tf_op jit(solution)/shard_map/squeeze | solution.py:70
  20.6 5.8 %gather_fusion.2 = bf16[1024,256]{1,0:T(8,128)(2,1)} fusion(bf16[1536,256]{1,0:T(8,128)(2,1)} %get-tuple-element.16, s32[1024]{0:T(1024)S(1)} %get-tuple-element.35), kind=kCustom, calls=%fused_computation.1.clone | custom fusion | bytes 1052672 | tf_op jit(solution)/shard_map/jit(_take)/gather | solution.py:70
  26.4 2.0 %reshape.155 = bf16[256,4,256]{2,1,0:T(4,128)(2,1)} reshape(bf16[1024,256]{1,0:T(8,128)(2,1)} %gather_fusion.2) | data formatting | bytes 1048576 | tf_op jit(solution)/shard_map/jit(_take)/gather | solution.py:70
  28.4 4.9 %gather_fusion.3 = bf16[1024,256]{1,0:T(8,128)(2,1)} fusion(bf16[1536,256]{1,0:T(8,128)(2,1)S(1)} %get-tuple-element.15, s32[1024]{0:T(1024)S(1)} %get-tuple-element.34), kind=kCustom, calls=%fused_computation.2.clone | custom fusion | bytes 1052672 | tf_op jit(solution)/shard_map/jit(_take)/gather | solution.py:70
  33.3 1.9 %reshape.159 = bf16[256,4,256]{2,1,0:T(4,128)(2,1)} reshape(bf16[1024,256]{1,0:T(8,128)(2,1)} %gather_fusion.3) | data formatting | bytes 1048576 | tf_op jit(solution)/shard_map/jit(_take)/gather | solution.py:70
  35.2 3.9 %gather_fusion.1 = bf16[1024,256]{1,0:T(8,128)(2,1)S(1)} fusion(bf16[1536,256]{1,0:T(8,128)(2,1)S(1)} %get-tuple-element.14, s32[1024]{0:T(1024)S(1)} %broadcast_clamp_fusion.2), kind=kCustom, calls=%fused_computation.clone | custom fusion | bytes 1052672 | tf_op jit(solution)/shard_map/jit(_take)/gather | solution.py:70
  39.3 1.3 %fusion.20 = bf16[256,1,4,256]{3,0,2,1:T(8,128)(2,1)S(1)} fusion(bf16[256,4,256]{2,1,0:T(4,128)(2,1)} %reshape.155, pred[256,4]{0,1:T(4,128)(4,1)} %get-tuple-element.23), kind=kLoop, calls=%fused_computation.27 | loop fusion | flops 262144 | bytes 1049600 | tf_op jit(solution)/shard_map/stack | solution.py:69
  40.6 0.9 %fusion.19 = bf16[256,1,4,256]{3,0,2,1:T(8,128)(2,1)S(1)} fusion(bf16[256,4,256]{2,1,0:T(4,128)(2,1)S(1)} %copy-done.2, pred[256,4]{0,1:T(4,128)(4,1)} %get-tuple-element.22), kind=kLoop, calls=%fused_computation.25 | loop fusion | flops 262144 | bytes 1049600 | tf_op jit(solution)/shard_map/stack | solution.py:69
  41.5 0.9 fusion.21
  42.4 1.6 %multiply_convert_fusion.1 = (bf16[256,256]{0,1:T(8,128)(2,1)S(1)}, bf16[256,256]{0,1:T(8,128)(2,1)S(1)}) fusion(f32[256,256]{0,1:T(8,128)S(1)} %copy-done.3, bf16[3,4,256,256]{3,2,1,0:T(8,128)(2,1)S(1)} %copy-done, bf16[256,1,4,256]{3,0,2,1:T(8,128)(2,1)S(1)} %fusion.19, bf16[256,1,4,256]{3,0,2,1:T(8,128)(2,1)S(1)} %fusion.20, ...), kind=kOutput, calls=%fused_computation.49 | convolution fusion | flops 404488192 | bytes 3670016 | tf_op jit(solution)/shard_map/dot_general | solution.py:75
  44.1 0.3 fusion.11
  44.4 0.3 copy-done.10
  44.9 0.6 fusion.43
  45.5 10.7 %all_gather.3 = bf16[2,2048]{1,0:T(2,128)(2,1)S(1)} all-gather(bf16[2,256]{1,0:T(2,128)(2,1)S(1)} %get-tuple-element.12), channel_id=1, replica_groups=mesh['grp'=4,'tile'=8] {'tile'}, dimensions={1}, use_global_device_ids=true | all-gather | bytes 9216 | tf_op jit(solution)/shard_map/all_gather | solution.py:91
  56.2 2.1 %gather_fusion = bf16[448,2,128]{2,1,0:T(2,128)(2,1)S(1)} fusion(bf16[2,16,128]{2,0,1:T(2,128)(2,1)S(1)} %bitcast.46, s32[1024]{0:T(1024)S(1)} %pad_clamp_fusion), kind=kCustom, calls=%fused_computation.3 | custom fusion | bytes 460544 | tf_op jit(solution)/shard_map/jit(_take)/gather | solution.py:94
  58.3 0.7 fusion.30
  59.0 3.6 %fusion = f32[112,1,16,1,1]{2,1,4,3,0:T(1,128)S(1)} fusion(bf16[112,4,16,2,128]{4,3,2,1,0:T(2,128)(2,1)} %param.15, bf16[2,112,4,128,1]{3,0,2,1,4:T(2,128)(2,1)S(1)} %fusion.30), kind=kOutput, calls=%fused_computation.4 | convolution fusion | flops 3670016 | bytes 3906560 | tf_op jit(solution)/shard_map/rjics,crjs->ri/dot_general | solution.py:95
  62.7 10.1 %psum.21 = f32[1792]{0:T(1024)S(1)} all-reduce(f32[1792]{0:T(1024)S(1)} %reshape.107), channel_id=1, replica_groups=mesh['grp'=4,'tile'=8] {'grp'}, use_global_device_ids=true, to_apply=%region_4.6 | all-reduce | flops 1792 | bytes 14336 | tf_op jit(solution)/shard_map/psum | solution.py:98
  72.9 13.6 %all-reduce = (f32[3]{0:T(128)S(1)}, f32[3]{0:T(128)S(1)}) all-reduce(f32[3]{0:T(128)S(1)} %get-tuple-element.7, f32[3]{0:T(128)S(1)} %get-tuple-element.6), channel_id=1, replica_groups=mesh['grp'=4,'tile'=8] {'tile'}, use_global_device_ids=true, to_apply=%region_6.8 | all-reduce | flops 6 | bytes 48 | tf_op jit(solution)/shard_map/psum | solution.py:100
  86.6 0.6 sub.58
  (50 shorter events, 1.9 us)
Async XLA Ops:
  0.6 41.8 %copy-start = (bf16[3,4,256,256]{3,2,1,0:T(8,128)(2,1)S(1)}, bf16[3,4,256,256]{3,2,1,0:T(8,128)(2,1)}, u32[]{:S(2)}) copy-start(bf16[3,4,256,256]{3,2,1,0:T(8,128)(2,1)} %param.12) | copy-start | bytes 4718596
  0.6 17.8 %copy-start.1 = (bf16[3,1024,256]{2,1,0:T(8,128)(2,1)S(1)}, bf16[3,1024,256]{2,1,0:T(8,128)(2,1)}, u32[]{:S(2)}) copy-start(bf16[3,1024,256]{2,1,0:T(8,128)(2,1)} %param.11) | copy-start | bytes 4718596
  0.7 12.7 %copy-start.11 = (s32[112,4]{0,1:T(4,128)S(1)}, s32[112,4]{0,1:T(4,128)}, u32[]{:S(2)}) copy-start(s32[112,4]{0,1:T(4,128)} %param.16) | copy-start | bytes 5380
  0.7 16.0 %copy-start.6 = (s32[1792]{0:T(1024)S(1)}, s32[1792]{0:T(1024)}, u32[]{:S(2)}) copy-start(s32[1792]{0:T(1024)} %param.18) | copy-start | bytes 21508
  0.7 16.0 %copy-start.12 = (f32[3]{0:T(128)S(1)}, f32[3]{0:T(128)}, u32[]{:S(2)}) copy-start(f32[3]{0:T(128)} %param.19) | copy-start | bytes 40
  2.9 14.5 %collective-permute-start = (bf16[3,256,256]{2,1,0:T(8,128)(2,1)}, bf16[3,256,256]{2,1,0:T(8,128)(2,1)}, u32[]{:S(2)}, u32[]{:S(2)}) collective-permute-start(bf16[3,256,256]{2,1,0:T(8,128)(2,1)} %get-tuple-element.18), channel_id=1, source_target_pairs={{31,0},{0,1},{1,2},{2,3},{3,4},{4,5},{5,6},{6,7},{7,8},{8,9},{9,10... | collective-permute-start | bytes 1179656 | tf_op jit(solution)/shard_map/ppermute | solution.py:14
  3.4 15.2 %collective-permute-start.1 = (bf16[3,256,256]{2,1,0:T(8,128)(2,1)}, bf16[3,256,256]{2,1,0:T(8,128)(2,1)}, u32[]{:S(2)}, u32[]{:S(2)}) collective-permute-start(bf16[3,256,256]{2,1,0:T(8,128)(2,1)} %get-tuple-element.17), channel_id=1, source_target_pairs={{1,0},{2,1},{3,2},{4,3},{5,4},{6,5},{7,6},{8,7},{9,8},{10,9},{11,1... | collective-permute-start | bytes 1179656 | tf_op jit(solution)/shard_map/ppermute | solution.py:14
  39.2 1.5 %copy-start.2 = (bf16[256,4,256]{2,1,0:T(4,128)(2,1)S(1)}, bf16[256,4,256]{2,1,0:T(4,128)(2,1)}, u32[]{:S(2)}) copy-start(bf16[256,4,256]{2,1,0:T(4,128)(2,1)} %reshape.159) | copy-start | bytes 1572868
  39.3 3.1 %copy-start.3 = (f32[256,256]{0,1:T(8,128)S(1)}, f32[256,256]{0,1:T(8,128)}, u32[]{:S(2)}) copy-start(f32[256,256]{0,1:T(8,128)} %copy.33) | copy-start | bytes 786436
  42.4 1.7 %copy-start.4 = (bf16[256,256]{1,0:T(8,128)(2,1)S(1)}, bf16[256,256]{1,0:T(8,128)(2,1)}, u32[]{:S(2)}) copy-start(bf16[256,256]{1,0:T(8,128)(2,1)} %get-tuple-element.28) | copy-start | bytes 393220
  42.4 1.7 %copy-start.5 = (bf16[256,256]{1,0:T(8,128)(2,1)S(1)}, bf16[256,256]{1,0:T(8,128)(2,1)}, u32[]{:S(2)}) copy-start(bf16[256,256]{1,0:T(8,128)(2,1)} %get-tuple-element.29) | copy-start | bytes 393220
  44.1 0.7 copy-start.10
  44.1 14.2 %copy-start.7 = (pred[112,4]{1,0:T(8,128)(4,1)S(1)}, pred[112,4]{1,0:T(8,128)(4,1)}, u32[]{:S(2)}) copy-start(pred[112,4]{1,0:T(8,128)(4,1)} %copy.35) | copy-start | bytes 1348
  59.0 13.8 %copy-start.8 = (f32[1792]{0:T(1024)S(1)}, f32[1792]{0:T(1024)}, u32[]{:S(2)}) copy-start(f32[1792]{0:T(1024)} %select_reduce_fusion.2) | copy-start | bytes 21508
  59.0 13.8 %copy-start.9 = (f32[1792]{0:T(1024)S(1)}, f32[1792]{0:T(1024)}, u32[]{:S(2)}) copy-start(f32[1792]{0:T(1024)} %param.17) | copy-start | bytes 21508
where the time goes:
time: 87.8 us; the launch traced here: 87.2 us
  blocking collectives  34.3 us (39%)
  local copies, waits for them, and re-layouts  30.1 us (34%)
  other arithmetic  9.87 us (11%)
  starting transfers between devices  6.37 us (7%)
  matrix products  5.54 us (6%)
  between operations  1.02 us (1%)
    gather x6, local copies, waits for them, and re-layouts, on_device(): jnp.take(extended[layer], local_ids[:, layer, :], axis=0)  18.7 us
    psum x1, blocking collectives, on_device(): total_sums, total_counts = lax.psum((sums, counts), 'tile')  13.6 us
    all_gather x1, blocking collectives, on_device(): gathered = lax.all_gather(slope_words, 'tile', axis=1, tiled=True)  10.7 us
    psum x1, blocking collectives, on_device(): recon = lax.psum(partial_value, 'grp')  10.1 us
    ppermute x2, starting transfers between devices, from_behind(): return lax.ppermute(block, axis, route)  6.37 us
    dot_general x1, matrix products, on_device(): jnp.einsum('rjics,crjs->ri', cm_values, chosen, preferred_element_type=jn...  3.61 us
    unnamed x29, local copies, waits for them, and re-layouts  3.29 us
    another operation x3, other arithmetic, on_device(): jnp.stack([jnp.take(extended[layer], local_ids[:, layer, :], axis=0) for...  3.03 us
  transfers between devices with their start and end apart: 2, of which 0 were waited for; matrix products, arithmetic and copies ran while one was open for 10% of the time, Pallas kernels for 0%

commit v1 on v0

v1 whole, which is shorter than its diff:
```python
import functools
import math

import jax
import jax.numpy as jnp
import numpy as np
from jax import lax
from jax.experimental import pallas as pl
from jax.experimental.pallas import tpu as pltpu
from jax.sharding import PartitionSpec as P

SIDE = 16
LANES = 128
GROUP = 8
MESH = pl.DeviceIdType.MESH


def transform_table(side):
    index = np.arange(side * side)
    row_ids, col_ids = index // side, index % side
    turns = (row_ids[:, None] * row_ids[None, :] + col_ids[:, None] * col_ids[None, :]) % side
    angle = turns.astype(np.float32) * np.float32(2.0 * math.pi / side)
    cosine, sine = np.cos(angle), np.sin(angle)
    table = np.concatenate(
        [np.concatenate([cosine, -sine], 1), np.concatenate([sine, cosine], 1)], 0
    )
    return jnp.asarray(table.T.astype(jnp.bfloat16))


def gather_table(nonzero, acts, comps):
    width = nonzero * acts * comps
    rows = np.arange(GROUP * width)
    target = (rows // width) * acts + (rows % (acts * comps)) // comps
    table = target[:, None] == np.arange(GROUP * acts)[None, :]
    return jnp.asarray(table.astype(jnp.bfloat16))


def cos_sin(x):
    turns = jnp.floor(x * np.float32(2.0 / math.pi) + 0.5)
    r = x - turns * np.float32(1.5703125)
    r = r - turns * np.float32(4.837512969970703125e-4)
    r = r - turns * np.float32(7.54978995489188216e-8)
    r2 = r * r
    s = np.float32(8.3321608736e-3) + r2 * np.float32(-1.9515295891e-4)
    s = np.float32(-1.6666654611e-1) + r2 * s
    s = r + r * r2 * s
    c = np.float32(-1.388731625493765e-3) + r2 * np.float32(2.443315711809948e-5)
    c = np.float32(4.166664568298827e-2) + r2 * c
    c = (1.0 - 0.5 * r2) + r2 * r2 * c
    quarter = turns.astype(jnp.int32)
    odd = (quarter & 1) == 1
    cosine = jnp.where(odd, s, c)
    sine = jnp.where(odd, c, s)
    cosine = jnp.where(((quarter + 1) & 2) == 2, -cosine, cosine)
    sine = jnp.where((quarter & 2) == 2, -sine, sine)
    return cosine, sine


def one_hot(column, base, width):
    ids = lax.broadcasted_iota(jnp.int32, (column.shape[0], width), 1)
    return jnp.where(column - base == ids, 1.0, 0.0).astype(jnp.bfloat16)


def step_kernel(
    grps,
    tiles,
    screens,
    weights,
    footprint,
    illum,
    cm,
    cols,
    prev,
    owner,
    gain,
    table,
    spread,
    slopes_out,
    commands_out,
    screens_v,
    halo,
    weights_v,
    foot_v,
    illum_v,
    cm_v,
    cols_v,
    prev_v,
    owner_v,
    gain_s,
    table_v,
    spread_v,
    picked,
    words,
    chosen,
    z_v,
    parts,
    sums,
    load_sem,
    screen_sem,
    halo_send,
    halo_recv,
    word_send,
    word_recv,
    part_send,
    part_recv,
    sum_send,
    sum_recv,
):
    layers, blk_dev, pixels = screens.shape
    foot = footprint.shape[1]
    sub_dev = illum.shape[0]
    reach = halo.shape[2]
    mirrors = gain.shape[0]
    per_dev = sub_dev // LANES
    rowblk = cm.shape[0]
    width = cm.shape[1]
    nonzero = cols.shape[0]
    acts = width // (2 * nonzero)
    rows = prev.shape[0]
    devices = grps * tiles
    my_grp = lax.axis_index("grp")
    my_tile = lax.axis_index("tile")
    me = my_grp * tiles + my_tile

    def place(device):
        return (device // tiles, device % tiles)

    barrier = pltpu.get_barrier_semaphore()

    def greet(offset, carry):
        pl.semaphore_signal(
            barrier,
            inc=1,
            device_id=place(lax.rem(me + offset, devices)),
            device_id_type=MESH,
        )
        return carry

    lax.fori_loop(1, devices, greet, 0)

    loads = {}
    for number, (name, src, dst) in enumerate(
        [
            ("foot", footprint, foot_v),
            ("weights", weights, weights_v),
            ("cols", cols, cols_v),
            ("gain", gain, gain_s),
            ("prev", prev, prev_v),
            ("owner", owner, owner_v),
            ("illum", illum, illum_v),
            ("table", table, table_v),
            ("spread", spread, spread_v),
            ("cm", cm, cm_v),
        ]
    ):
        loads[name] = pltpu.make_async_copy(src, dst, load_sem.at[number])
    screen_loads = [
        pltpu.make_async_copy(screens.at[layer], screens_v.at[layer], screen_sem.at[layer])
        for layer in range(layers)
    ]
    loads["foot"].start()
    for load in screen_loads:
        load.start()
    for name in loads:
        if name != "foot":
            loads[name].start()

    pl.semaphore_wait(barrier, devices - 1)

    last = lax.rem(me + devices - 1, devices)
    following = lax.rem(me + 1, devices)
    halo_copies = []
    for layer in range(layers):
        for side, (first, target) in enumerate([(blk_dev - reach, following), (0, last)]):
            copy = pltpu.make_async_remote_copy(
                src_ref=screens.at[layer, pl.ds(first, reach)],
                dst_ref=halo.at[layer, side],
                send_sem=halo_send.at[layer, side],
                recv_sem=halo_recv.at[layer, side],
                device_id=place(target),
                device_id_type=MESH,
            )
            copy.start()
            halo_copies.append(copy)

    loads["foot"].wait()
    columns = []
    for layer in range(layers):
        local = foot_v[layer] - (me * blk_dev - reach)
        local = jnp.where(local < 0, local + blk_dev * devices, local)
        local = jnp.where(local >= blk_dev * devices, local - blk_dev * devices, local)
        flipped = jnp.transpose(local)
        columns.append([flipped[:, k : k + 1] for k in range(foot)])

    for layer in range(layers):
        screen_loads[layer].wait()
        for k in range(foot):
            mine = jnp.dot(
                one_hot(columns[layer][k], reach, blk_dev),
                screens_v[layer],
                preferred_element_type=jnp.float32,
            )
            picked[layer, k] = mine.astype(jnp.bfloat16)

    loads["cols"].wait()
    lanes = lax.broadcasted_iota(jnp.int32, (rowblk, width), 1)
    col_ids = jnp.transpose(cols_v[...] - my_grp * (tiles * per_dev))
    code = jnp.zeros((rowblk, width), jnp.int32)
    for n in range(nonzero):
        code = jnp.where(
            lanes // (acts * 2) == n, jnp.broadcast_to(col_ids[:, n : n + 1], code.shape), code
        )
    code = ((code // per_dev) * 2 + lanes % 2) * per_dev + code % per_dev

    loads["gain"].wait()
    loads["owner"].wait()
    loads["prev"].wait()
    owners = owner_v[...]
    gains = jnp.zeros(owners.shape, jnp.float32)
    for m in range(mirrors):
        gains = jnp.where(owners == m, gain_s[m], gains)

    for name in ("weights", "illum", "table", "spread", "cm"):
        loads[name].wait()

    phase = jnp.zeros((sub_dev, pixels), jnp.float32)
    for layer in range(layers):
        for side in range(2):
            halo_copies[2 * layer + side].wait_recv()
        around = halo[layer].reshape(2 * reach, pixels)
        for k in range(foot):
            column = columns[layer][k]
            hot = jnp.concatenate(
                [one_hot(column, 0, reach), one_hot(column, reach + blk_dev, reach)], 1
            )
            other = jnp.dot(hot, around, preferred_element_type=jnp.float32)
            both = picked[layer, k] + other.astype(jnp.bfloat16)
            phase += jnp.dot(
                both, weights_v[layer * foot + k], preferred_element_type=jnp.float32
            )

    cosine, sine = cos_sin(phase)
    bright = illum_v[...]
    field = jnp.concatenate([bright * cosine, bright * sine], 1).astype(jnp.bfloat16)
    spectrum = lax.dot_general(
        table_v[...], field, (((1,), (1,)), ((), ())), preferred_element_type=jnp.float32
    )
    real_part, imag_part = spectrum[:pixels], spectrum[pixels:]
    intensity = real_part * real_part + imag_part * imag_part
    freq = lax.broadcasted_iota(jnp.int32, (pixels, sub_dev), 0)
    half = SIDE // 2
    freq_v, freq_u = freq % SIDE, freq // SIDE
    centre_v = (freq_v - jnp.where(freq_v >= half, SIDE, 0)).astype(jnp.float32)
    centre_u = (freq_u - jnp.where(freq_u >= half, SIDE, 0)).astype(jnp.float32)
    total = jnp.sum(intensity, axis=0, keepdims=True)
    slope_x = jnp.sum(intensity * centre_v, axis=0, keepdims=True) / total
    slope_y = jnp.sum(intensity * centre_u, axis=0, keepdims=True) / total
    slopes_out[0:1, :] = slope_x
    slopes_out[1:2, :] = slope_y
    for c, slope in enumerate((slope_x, slope_y)):
        for b in range(per_dev):
            words[my_tile, pl.ds(c * per_dev + b, 1), :] = slope[:, b * LANES : (b + 1) * LANES]

    word_copies = []
    for offset in range(1, tiles):
        copy = pltpu.make_async_remote_copy(
            src_ref=words.at[my_tile],
            dst_ref=words.at[my_tile],
            send_sem=word_send.at[offset],
            recv_sem=word_recv.at[offset],
            device_id=(my_grp, lax.rem(my_tile + offset, tiles)),
            device_id_type=MESH,
        )
        copy.start()
        word_copies.append(copy)
    for copy in word_copies:
        copy.wait_recv()

    height = 2 * per_dev
    for d in range(tiles):
        chosen[d * height : (d + 1) * height, :] = words[d]
    stack = chosen[...].astype(jnp.bfloat16)
    place_ids = lax.broadcasted_iota(jnp.int32, (tiles * height, width), 0)
    z_v[...] = jnp.zeros(z_v.shape, jnp.float32)
    for start in range(0, rowblk, GROUP):
        count = min(GROUP, rowblk - start)
        values = cm_v[start : start + count].reshape(count * width, LANES)
        product = lax.dot_general(
            stack, values, (((1,), (1,)), ((), ())), preferred_element_type=jnp.float32
        )
        for r in range(count):
            wanted = place_ids == code[start + r : start + r + 1, :]
            kept = jnp.where(wanted, product[:, r * width : (r + 1) * width], 0.0)
            z_v[start + r : start + r + 1, :] = jnp.sum(kept, axis=0, keepdims=True)
    out_rows = z_v.shape[0] // GROUP
    wide = jnp.concatenate([z_v[pl.ds(r, out_rows, stride=GROUP), :] for r in range(GROUP)], 1)
    high = wide.astype(jnp.bfloat16)
    rest = wide - high.astype(jnp.float32)
    middle = rest.astype(jnp.bfloat16)
    low = (rest - middle.astype(jnp.float32)).astype(jnp.bfloat16)
    folded = jnp.dot(
        jnp.concatenate([high, middle, low], 0), spread_v[...], preferred_element_type=jnp.float32
    )
    partial = folded[:out_rows] + (folded[out_rows : 2 * out_rows] + folded[2 * out_rows :])

    previous = prev_v[...]
    first_grp = jnp.where(my_grp == 0, 1.0, 0.0).astype(jnp.float32)
    moved = first_grp * previous - gains * partial[:rows]
    lines = []
    for m in range(mirrors):
        lines.append(jnp.sum(jnp.where(owners == m, moved, 0.0), axis=0, keepdims=True))
    for m in range(mirrors):
        lines.append(jnp.sum(jnp.where(owners == m, first_grp, 0.0), axis=0, keepdims=True))
    parts[my_grp] = partial
    for number, line in enumerate(lines):
        sums[me, pl.ds(number, 1), :] = line
    for number in range(len(lines), sums.shape[1]):
        sums[me, pl.ds(number, 1), :] = jnp.zeros((1, LANES), jnp.float32)

    part_copies = []
    for offset in range(1, grps):
        copy = pltpu.make_async_remote_copy(
            src_ref=parts.at[my_grp],
            dst_ref=parts.at[my_grp],
            send_sem=part_send.at[offset],
            recv_sem=part_recv.at[offset],
            device_id=(lax.rem(my_grp + offset, grps), my_tile),
            device_id_type=MESH,
        )
        copy.start()
        part_copies.append(copy)

    def sum_copy(offset):
        return pltpu.make_async_remote_copy(
            src_ref=sums.at[me],
            dst_ref=sums.at[me],
            send_sem=sum_send.at[offset],
            recv_sem=sum_recv.at[offset],
            device_id=place(lax.rem(me + offset, devices)),
            device_id_type=MESH,
        )

    def send_sum(offset, carry):
        sum_copy(offset).start()
        return carry

    def take_sum(offset, carry):
        sum_copy(offset).wait_recv()
        return carry

    def leave_sum(offset, carry):
        sum_copy(offset).wait_send()
        return carry

    lax.fori_loop(1, devices, send_sum, 0)
    for copy in part_copies:
        copy.wait_recv()
    recon = parts[0]
    for g in range(1, grps):
        recon = recon + parts[g]
    updated = previous - gains * recon[:rows]
    lax.fori_loop(1, devices, take_sum, 0)
    everything = jnp.sum(jnp.sum(sums[...], axis=0), axis=1, keepdims=True)
    piston = jnp.zeros(owners.shape, jnp.float32)
    for m in range(mirrors):
        mean = everything[m : m + 1] / everything[mirrors + m : mirrors + m + 1]
        piston = jnp.where(owners == m, mean, piston)
    commands_out[...] = updated - piston

    for copy in halo_copies + word_copies + part_copies:
        copy.wait_send()
    lax.fori_loop(1, devices, leave_sum, 0)


def on_device(
    screens,
    interp_weights,
    footprint,
    illumination,
    cm_values,
    cm_columns,
    prev_commands,
    owner_map,
    dm_gain,
):
    grps, tiles = lax.axis_size("grp"), lax.axis_size("tile")
    devices = grps * tiles
    layers, blk_dev, pixels = screens.shape
    sub_dev = illumination.shape[0]
    foot = footprint.shape[2]
    reach = blk_dev // 4
    rowblk, nonzero, acts, comps, cbs = cm_values.shape
    width = nonzero * acts * comps
    act_dev = prev_commands.shape[0]
    mirrors = dm_gain.shape[0]
    per_dev = sub_dev // cbs
    rows = -(-act_dev // LANES)
    spare = rows * LANES - act_dev
    if spare:
        prev_commands = jnp.pad(prev_commands, (0, spare))
        owner_map = jnp.pad(owner_map, (0, spare), constant_values=-1)
    out_rows = -(-rows // 16) * 16
    sum_rows = -(-2 * mirrors // 8) * 8
    table = transform_table(SIDE)
    spread = gather_table(nonzero, acts, comps)
    operands = (
        screens,
        interp_weights.reshape(layers * foot, pixels, pixels),
        jnp.transpose(footprint, (1, 2, 0)),
        illumination,
        cm_values.reshape(rowblk, width, cbs),
        jnp.transpose(cm_columns),
        prev_commands.reshape(rows, LANES),
        owner_map.reshape(rows, LANES),
        dm_gain,
        table,
        spread,
    )
    scratch = [pltpu.VMEM(screens.shape, screens.dtype)]
    scratch.append(pltpu.VMEM((layers, 2, reach, pixels), screens.dtype))
    for position in (1, 2, 3, 4, 5, 6, 7):
        scratch.append(pltpu.VMEM(operands[position].shape, operands[position].dtype))
    scratch.append(pltpu.SMEM(dm_gain.shape, dm_gain.dtype))
    for position in (9, 10):
        scratch.append(pltpu.VMEM(operands[position].shape, operands[position].dtype))
    scratch += [
        pltpu.VMEM((layers, foot, sub_dev, pixels), jnp.bfloat16),
        pltpu.VMEM((tiles, comps * per_dev, cbs), jnp.float32),
        pltpu.VMEM((tiles * comps * per_dev, cbs), jnp.float32),
        pltpu.VMEM((out_rows * GROUP, width), jnp.float32),
        pltpu.VMEM((grps, out_rows, LANES), jnp.float32),
        pltpu.VMEM((devices, sum_rows, LANES), jnp.float32),
        pltpu.SemaphoreType.DMA((10,)),
        pltpu.SemaphoreType.DMA((layers,)),
        pltpu.SemaphoreType.DMA((layers, 2)),
        pltpu.SemaphoreType.DMA((layers, 2)),
        pltpu.SemaphoreType.DMA((tiles,)),
        pltpu.SemaphoreType.DMA((tiles,)),
        pltpu.SemaphoreType.DMA((grps,)),
        pltpu.SemaphoreType.DMA((grps,)),
        pltpu.SemaphoreType.DMA((devices,)),
        pltpu.SemaphoreType.DMA((devices,)),
    ]
    slopes, commands = pl.pallas_call(
        functools.partial(step_kernel, grps, tiles),
        out_shape=(
            jax.ShapeDtypeStruct((comps, sub_dev), jnp.float32),
            jax.ShapeDtypeStruct((rows, LANES), jnp.float32),
        ),
        in_specs=[pl.BlockSpec(memory_space=pl.ANY)] * len(operands),
        out_specs=(
            pl.BlockSpec(memory_space=pltpu.VMEM),
            pl.BlockSpec(memory_space=pltpu.VMEM),
        ),
        scratch_shapes=scratch,
        compiler_params=pltpu.CompilerParams(
            collective_id=0, has_side_effects=True, vmem_limit_bytes=56 * 1024 * 1024
        ),
    )(*operands)
    return (slopes, commands.reshape(-1)[:act_dev])


def solution(mesh):
    in_specs = (
        P(None, ("grp", "tile"), None),
        P(),
        P(("grp", "tile"), None, None),
        P(("grp", "tile"), None),
        P("tile", "grp", None, None, None),
        P("tile", "grp"),
        P("tile"),
        P("tile"),
        P(),
    )
    out_specs = (P(None, ("grp", "tile")), P("tile"))
    return jax.shard_map(
        on_device, mesh=mesh, in_specs=in_specs, out_specs=out_specs, check_vma=False
    )
```

time: 87.8 us -> 35 us (0.40)
  blocking collectives: 34.3 us -> 0 us
  Pallas kernels: 0 us -> 31.6 us
  local copies, waits for them, and re-layouts: 30.1 us -> 2.53 us
  other arithmetic: 9.87 us -> 0 us
  starting transfers between devices: 6.37 us -> 0 us
  matrix products: 5.54 us -> 0 us
    pallas_call x0 -> x1, Pallas kernels: none -> 31.6 us  [on_device(): pl.pallas_call(functools.partial(step_kernel, grps, tiles), out_shape=(ja...]
    psum x2 -> x0, blocking collectives: 23.7 us -> none  [the longest x1 13.6 us: on_device(): total_sums, total_counts = lax.psum((sums, counts), 'tile')]
    gather x7 -> x0, local copies, waits for them, and re-layouts: 20.8 us -> none  [the longest x6 18.7 us: on_device(): jnp.take(extended[layer], local_ids[:, layer, :], axis=0)]
    all_gather x1 -> x0, blocking collectives: 10.7 us -> none  [on_device(): gathered = lax.all_gather(slope_words, 'tile', axis=1, tiled=True)]
    ppermute x2 -> x0, starting transfers between devices: 6.37 us -> none  [from_behind(): return lax.ppermute(block, axis, route)]
    dot_general x3 -> x0, matrix products: 5.54 us -> none  [the longest x1 3.61 us: on_device(): jnp.einsum('rjics,crjs->ri', cm_values, chosen, preferred_element_type=jn...]
    another operation x4 -> x0, other arithmetic: 4.97 us -> none  [the longest x3 3.03 us: on_device(): jnp.stack([jnp.take(extended[layer], local_ids[:, layer, :], axis=0) for...]
    slice x1 -> x0, local copies, waits for them, and re-layouts: 2.21 us -> none  [on_device(): after = from_behind(screens[:, :reach, :], ('grp', 'tile'), -1)]
  transfers between devices with their start and end apart: 2 -> 0, of which waited for: 0 -> 0; matrix products, arithmetic and copies ran while one was open for 10% -> 0% of each run, Pallas kernels for 0% -> 0%
where the time goes in v1:
time: 35 us; the launch traced here: 34.8 us
  Pallas kernels  31.6 us (90%)
  local copies, waits for them, and re-layouts  2.53 us (7%)
  between operations  0.64 us (2%)
    pallas_call x1, Pallas kernels, on_device(): pl.pallas_call(functools.partial(step_kernel, grps, tiles), out_shape=(ja...  31.6 us
    unnamed x2, local copies, waits for them, and re-layouts  2.53 us

profile of v1, /device:TPU:0, one launch (start us, length us, event | category | flops | bytes accessed | tf_op | source)
XLA Modules:
  0.0 34.8 jit_solution(5937664595378733878)
XLA Ops:
  0.6 31.6 %shard_map.122 = (f32[2,256]{1,0:T(2,128)}, f32[14,128]{1,0:T(8,128)}) custom-call(bf16[3,1024,256]{2,1,0:T(8,128)(2,1)} %screens.1, bf16[12,256,256]{2,1,0:T(8,128)(2,1)} %bitcast.8, s32[3,4,256]{2,1,0:T(4,128)} %bitcast.9, f32[256,256]{1,0:T(8,128)} %illum.1, bf16[112,128,128]{2,1,0:T(8,128)(2,1)} %bitcast.7, s32[4,112]{1,0:T(4,128)} %bitcast.13, ...), custom_call_target="tpu_custom_call" | custom-call | tf_op jit(solution)/shard_map/pallas_call | solution.py:444
  32.2 1.2 %copy.15 = f32[2,256]{1,0:T(2,128)} copy(f32[2,256]{1,0:T(2,128)} %get-tuple-element.8) | data formatting | bytes 4096
  33.5 1.3 %copy.16 = f32[1792]{0:T(1024)} copy(f32[1792]{0:T(1024)} %bitcast.12) | data formatting | bytes 14336

commit v2 on v1

v2 whole, which is shorter than its diff:
```python
import functools
import math

import jax
import jax.numpy as jnp
import numpy as np
from jax import lax
from jax.experimental import pallas as pl
from jax.experimental.pallas import tpu as pltpu
from jax.sharding import PartitionSpec as P

SIDE = 16
LANES = 128
SUBLANES = 8
MESH = pl.DeviceIdType.MESH


def transform_table(side):
    index = np.arange(side * side)
    row_ids, col_ids = index // side, index % side
    turns = (row_ids[:, None] * row_ids[None, :] + col_ids[:, None] * col_ids[None, :]) % side
    angle = turns.astype(np.float32) * np.float32(2.0 * math.pi / side)
    cosine, sine = np.cos(angle), np.sin(angle)
    table = np.concatenate(
        [np.concatenate([cosine, -sine], 1), np.concatenate([sine, cosine], 1)], 0
    )
    return jnp.asarray(table.T.astype(jnp.bfloat16))


def cos_sin(x):
    turns = jnp.floor(x * np.float32(2.0 / math.pi) + 0.5)
    r = x - turns * np.float32(1.5703125)
    r = r - turns * np.float32(4.837512969970703125e-4)
    r = r - turns * np.float32(7.54978995489188216e-8)
    r2 = r * r
    s = np.float32(8.3321608736e-3) + r2 * np.float32(-1.9515295891e-4)
    s = np.float32(-1.6666654611e-1) + r2 * s
    s = r + r * r2 * s
    c = np.float32(-1.388731625493765e-3) + r2 * np.float32(2.443315711809948e-5)
    c = np.float32(4.166664568298827e-2) + r2 * c
    c = (1.0 - 0.5 * r2) + r2 * r2 * c
    quarter = turns.astype(jnp.int32)
    odd = (quarter & 1) == 1
    cosine = jnp.where(odd, s, c)
    sine = jnp.where(odd, c, s)
    cosine = jnp.where(((quarter + 1) & 2) == 2, -cosine, cosine)
    sine = jnp.where((quarter & 2) == 2, -sine, sine)
    return cosine, sine


def one_hot(column, base, width):
    ids = lax.broadcasted_iota(jnp.int32, (column.shape[0], width), 1)
    return jnp.where(column - base == ids, 1.0, 0.0).astype(jnp.bfloat16)


def step_kernel(
    grps,
    tiles,
    screens,
    weights,
    footprint,
    illum,
    cm,
    cols,
    prev,
    owner,
    gain,
    table,
    slopes_out,
    commands_out,
    screens_v,
    halo,
    weights_v,
    foot_v,
    illum_v,
    cm_v,
    prev_v,
    owner_v,
    table_v,
    cols_s,
    gain_s,
    picked,
    far_hot,
    wide_cm,
    words,
    parts,
    sums,
    load_sem,
    screen_sem,
    halo_send,
    halo_recv,
    word_send,
    word_recv,
    part_send,
    part_recv,
    sum_send,
    sum_recv,
):
    layers, blk_dev, pixels = screens.shape
    foot = footprint.shape[1]
    sub_dev = illum.shape[0]
    reach = halo.shape[2]
    mirrors = gain.shape[0]
    per_dev = sub_dev // LANES
    rowblk, nonzero, tall = wide_cm.shape[:3]
    acts = tall * SUBLANES // 2
    rows = prev.shape[0]
    per_row = LANES // acts
    devices = grps * tiles
    my_grp = lax.axis_index("grp")
    my_tile = lax.axis_index("tile")
    me = my_grp * tiles + my_tile
    odd = lax.rem(me, 2)

    def place(device):
        return (device // tiles, device % tiles)

    barrier = pltpu.get_barrier_semaphore()

    def greet(offset, carry):
        pl.semaphore_signal(
            barrier,
            inc=1,
            device_id=place(lax.rem(me + offset, devices)),
            device_id_type=MESH,
        )
        return carry

    lax.fori_loop(1, devices, greet, 0)

    loads = {}
    for number, (name, src, dst) in enumerate(
        [
            ("foot", footprint, foot_v),
            ("weights", weights, weights_v),
            ("cols", cols, cols_s),
            ("gain", gain, gain_s),
            ("prev", prev, prev_v),
            ("owner", owner, owner_v),
            ("illum", illum, illum_v),
            ("table", table, table_v),
            ("cm", cm, cm_v),
        ]
    ):
        loads[name] = pltpu.make_async_copy(src, dst, load_sem.at[number])
    screen_loads = [
        pltpu.make_async_copy(screens.at[layer], screens_v.at[layer], screen_sem.at[layer])
        for layer in range(layers)
    ]
    loads["foot"].start()
    for load in screen_loads:
        load.start()
    for name in loads:
        if name != "foot":
            loads[name].start()

    pl.semaphore_wait(barrier, devices - 1)

    edge = blk_dev - reach
    far_copies, near_copies = [], []
    for kind, copies in enumerate((far_copies, near_copies)):
        ahead = odd if kind == 0 else 1 - odd
        target = place(lax.rem(me + devices + 2 * ahead - 1, devices))
        for layer in range(layers):
            copy = pltpu.make_async_remote_copy(
                src_ref=screens.at[layer, pl.ds(pl.multiple_of(edge * ahead, reach), reach)],
                dst_ref=halo.at[layer, kind],
                send_sem=halo_send.at[layer, kind],
                recv_sem=halo_recv.at[layer, kind],
                device_id=target,
                device_id_type=MESH,
            )
            copy.start()
            copies.append(copy)

    loads["foot"].wait()
    columns = []
    for layer in range(layers):
        local = foot_v[layer] - (me * blk_dev - reach)
        local = jnp.where(local < 0, local + blk_dev * devices, local)
        local = jnp.where(local >= blk_dev * devices, local - blk_dev * devices, local)
        flipped = jnp.transpose(local)
        columns.append([flipped[:, k : k + 1] for k in range(foot)])

    for layer in range(layers):
        screen_loads[layer].wait()
        for k in range(foot):
            mine = jnp.dot(
                one_hot(columns[layer][k], reach, blk_dev),
                screens_v[layer],
                preferred_element_type=jnp.float32,
            )
            picked[layer, k] = mine.astype(jnp.bfloat16)

    past = reach + blk_dev
    far_base, near_base = odd * past, (1 - odd) * past
    loads["weights"].wait()
    phase = jnp.zeros((sub_dev, pixels), jnp.float32)
    for layer in range(layers):
        near_copies[layer].wait_recv()
        for k in range(foot):
            column = columns[layer][k]
            near = jnp.dot(
                one_hot(column, near_base, reach),
                halo[layer, 1],
                preferred_element_type=jnp.float32,
            )
            both = picked[layer, k] + near.astype(jnp.bfloat16)
            phase += jnp.dot(
                both, weights_v[layer * foot + k], preferred_element_type=jnp.float32
            )
            far_hot[layer, k] = one_hot(column, far_base, reach)

    loads["cm"].wait()

    def widen(i, carry):
        wide_cm[i] = cm_v[i].astype(jnp.float32).reshape(wide_cm.shape[1:])
        return carry

    lax.fori_loop(0, rowblk, widen, 0)

    for name in ("cols", "gain", "owner", "prev", "illum", "table"):
        loads[name].wait()
    owners = owner_v[...]
    previous = prev_v[...]
    gains = jnp.zeros(owners.shape, jnp.float32)
    for m in range(mirrors):
        gains = jnp.where(owners == m, gain_s[m], gains)
    first_grp = jnp.where(my_grp == 0, 1.0, 0.0).astype(jnp.float32)

    for layer in range(layers):
        far_copies[layer].wait_recv()
        other = jnp.dot(
            far_hot[layer].reshape(foot * sub_dev, reach),
            halo[layer, 0],
            preferred_element_type=jnp.float32,
        ).astype(jnp.bfloat16)
        for k in range(foot):
            phase += jnp.dot(
                other[k * sub_dev : (k + 1) * sub_dev],
                weights_v[layer * foot + k],
                preferred_element_type=jnp.float32,
            )

    cosine, sine = cos_sin(phase)
    bright = illum_v[...]
    field = jnp.concatenate([bright * cosine, bright * sine], 1).astype(jnp.bfloat16)
    spectrum = lax.dot_general(
        table_v[...], field, (((1,), (1,)), ((), ())), preferred_element_type=jnp.float32
    )
    real_part, imag_part = spectrum[:pixels], spectrum[pixels:]
    intensity = real_part * real_part + imag_part * imag_part
    freq = lax.broadcasted_iota(jnp.int32, (pixels, sub_dev), 0)
    half = SIDE // 2
    freq_v, freq_u = freq % SIDE, freq // SIDE
    centre_v = (freq_v - jnp.where(freq_v >= half, SIDE, 0)).astype(jnp.float32)
    centre_u = (freq_u - jnp.where(freq_u >= half, SIDE, 0)).astype(jnp.float32)
    total = jnp.sum(intensity, axis=0, keepdims=True)
    slope_x = jnp.sum(intensity * centre_v, axis=0, keepdims=True) / total
    slope_y = jnp.sum(intensity * centre_u, axis=0, keepdims=True) / total
    tile_row = lax.broadcasted_iota(jnp.int32, (SUBLANES, sub_dev), 0)
    turned = jnp.where(
        tile_row % 2 == 0,
        jnp.broadcast_to(slope_x, tile_row.shape),
        jnp.broadcast_to(slope_y, tile_row.shape),
    )
    turned = turned.astype(jnp.bfloat16).astype(jnp.float32)
    for b in range(per_dev):
        words[my_tile * per_dev + b] = turned[:, b * LANES : (b + 1) * LANES]

    word_copies = []
    mine = pl.ds(my_tile * per_dev, per_dev)
    for offset in range(1, tiles):
        copy = pltpu.make_async_remote_copy(
            src_ref=words.at[mine],
            dst_ref=words.at[mine],
            send_sem=word_send.at[offset],
            recv_sem=word_recv.at[offset],
            device_id=(my_grp, lax.rem(my_tile + offset, tiles)),
            device_id_type=MESH,
        )
        copy.start()
        word_copies.append(copy)
    slopes_out[0:1, :] = slope_x
    slopes_out[1:2, :] = slope_y
    for copy in word_copies:
        copy.wait_recv()

    base_col = my_grp * (tiles * per_dev)
    act_row = (
        lax.broadcasted_iota(jnp.int32, (tall, SUBLANES, LANES), 0) * SUBLANES
        + lax.broadcasted_iota(jnp.int32, (tall, SUBLANES, LANES), 1)
    ) // 2
    lane = lax.broadcasted_iota(jnp.int32, (tall, SUBLANES, LANES), 2)
    for row in range(rows):
        spread = jnp.zeros((tall, SUBLANES, LANES), jnp.float32)
        for r in range(min(per_row, rowblk - row * per_row)):
            i = row * per_row + r
            products = jnp.zeros((tall, SUBLANES, LANES), jnp.float32)
            for n in range(nonzero):
                block = words[jnp.maximum(cols_s[n, i] - base_col, 0)]
                products = products + wide_cm[i, n] * block[None]
            reduced = jnp.sum(products, axis=2, keepdims=True)
            spread = jnp.where(lane == r * acts + act_row, reduced, spread)
        line = jnp.sum(jnp.sum(spread, axis=0), axis=0, keepdims=True)
        parts[my_grp, row : row + 1, :] = line
    partial = parts[my_grp]

    moved = first_grp * previous - gains * partial
    lines = []
    for m in range(mirrors):
        lines.append(jnp.sum(jnp.where(owners == m, moved, 0.0), axis=0, keepdims=True))
    for m in range(mirrors):
        lines.append(jnp.sum(jnp.where(owners == m, first_grp, 0.0), axis=0, keepdims=True))
    sum_row = lax.broadcasted_iota(jnp.int32, sums.shape[1:], 0)
    packed = jnp.zeros(sums.shape[1:], jnp.float32)
    for number, line in enumerate(lines):
        packed = jnp.where(sum_row == number, jnp.broadcast_to(line, packed.shape), packed)
    sums[me] = packed

    part_copies = []
    for offset in range(1, grps):
        copy = pltpu.make_async_remote_copy(
            src_ref=parts.at[my_grp],
            dst_ref=parts.at[my_grp],
            send_sem=part_send.at[offset],
            recv_sem=part_recv.at[offset],
            device_id=(lax.rem(my_grp + offset, grps), my_tile),
            device_id_type=MESH,
        )
        copy.start()
        part_copies.append(copy)

    def send_sum(offset, carry):
        pltpu.make_async_remote_copy(
            src_ref=sums.at[me],
            dst_ref=sums.at[me],
            send_sem=sum_send.at[0],
            recv_sem=sum_recv.at[0],
            device_id=place(lax.rem(me + offset, devices)),
            device_id_type=MESH,
        ).start()
        return carry

    lax.fori_loop(1, devices, send_sum, 0)
    others = sums.at[pl.ds(0, devices - 1)]
    for copy in part_copies:
        copy.wait_recv()
    recon = parts[0]
    for g in range(1, grps):
        recon = recon + parts[g]
    updated = previous - gains * recon
    pltpu.make_async_copy(others, others, sum_recv.at[0]).wait()
    everything = jnp.sum(jnp.sum(sums[...], axis=0), axis=1, keepdims=True)
    piston = jnp.zeros(owners.shape, jnp.float32)
    for m in range(mirrors):
        mean = everything[m : m + 1] / everything[mirrors + m : mirrors + m + 1]
        piston = jnp.where(owners == m, mean, piston)
    commands_out[...] = updated - piston

    for copy in far_copies + near_copies + word_copies + part_copies:
        copy.wait_send()
    pltpu.make_async_copy(others, others, sum_send.at[0]).wait()


def on_device(
    screens,
    interp_weights,
    footprint,
    illumination,
    cm_values,
    cm_columns,
    prev_commands,
    owner_map,
    dm_gain,
):
    grps, tiles = lax.axis_size("grp"), lax.axis_size("tile")
    devices = grps * tiles
    layers, blk_dev, pixels = screens.shape
    sub_dev = illumination.shape[0]
    foot = footprint.shape[2]
    reach = blk_dev // 4
    rowblk, nonzero, acts, comps, cbs = cm_values.shape
    width = nonzero * acts * comps
    act_dev = prev_commands.shape[0]
    mirrors = dm_gain.shape[0]
    per_dev = sub_dev // cbs
    rows = -(-act_dev // LANES)
    spare = rows * LANES - act_dev
    if spare:
        prev_commands = jnp.pad(prev_commands, (0, spare))
        owner_map = jnp.pad(owner_map, (0, spare), constant_values=-1)
    sum_rows = -(-2 * mirrors // SUBLANES) * SUBLANES
    operands = (
        screens,
        interp_weights.reshape(layers * foot, pixels, pixels),
        jnp.transpose(footprint, (1, 2, 0)),
        illumination,
        cm_values.reshape(rowblk, width, cbs),
        jnp.transpose(cm_columns),
        prev_commands.reshape(rows, LANES),
        owner_map.reshape(rows, LANES),
        dm_gain,
        transform_table(SIDE),
    )
    scratch = [pltpu.VMEM(screens.shape, screens.dtype)]
    scratch.append(pltpu.VMEM((layers, 2, reach, pixels), screens.dtype))
    for position in (1, 2, 3, 4, 6, 7, 9):
        scratch.append(pltpu.VMEM(operands[position].shape, operands[position].dtype))
    for position in (5, 8):
        scratch.append(pltpu.SMEM(operands[position].shape, operands[position].dtype))
    scratch += [
        pltpu.VMEM((layers, foot, sub_dev, pixels), jnp.bfloat16),
        pltpu.VMEM((layers, foot, sub_dev, reach), jnp.bfloat16),
        pltpu.VMEM((rowblk, nonzero, acts * comps // SUBLANES, SUBLANES, cbs), jnp.float32),
        pltpu.VMEM((tiles * per_dev, SUBLANES, cbs), jnp.float32),
        pltpu.VMEM((grps, rows, LANES), jnp.float32),
        pltpu.VMEM((devices, sum_rows, LANES), jnp.float32),
        pltpu.SemaphoreType.DMA((9,)),
        pltpu.SemaphoreType.DMA((layers,)),
        pltpu.SemaphoreType.DMA((layers, 2)),
        pltpu.SemaphoreType.DMA((layers, 2)),
        pltpu.SemaphoreType.DMA((tiles,)),
        pltpu.SemaphoreType.DMA((tiles,)),
        pltpu.SemaphoreType.DMA((grps,)),
        pltpu.SemaphoreType.DMA((grps,)),
        pltpu.SemaphoreType.DMA((1,)),
        pltpu.SemaphoreType.DMA((1,)),
    ]
    slopes, commands = pl.pallas_call(
        functools.partial(step_kernel, grps, tiles),
        out_shape=(
            pltpu.VMEM((comps, sub_dev), jnp.float32),
            pltpu.VMEM((rows, LANES), jnp.float32),
        ),
        in_specs=[pl.BlockSpec(memory_space=pl.ANY)] * len(operands),
        out_specs=(
            pl.BlockSpec(memory_space=pltpu.VMEM),
            pl.BlockSpec(memory_space=pltpu.VMEM),
        ),
        scratch_shapes=scratch,
        compiler_params=pltpu.CompilerParams(
            collective_id=0, has_side_effects=True, vmem_limit_bytes=56 * 1024 * 1024
        ),
    )(*operands)
    return (slopes, commands.reshape(-1)[:act_dev])


def solution(mesh):
    in_specs = (
        P(None, ("grp", "tile"), None),
        P(),
        P(("grp", "tile"), None, None),
        P(("grp", "tile"), None),
        P("tile", "grp", None, None, None),
        P("tile", "grp"),
        P("tile"),
        P("tile"),
        P(),
    )
    out_specs = (P(None, ("grp", "tile")), P("tile"))
    return jax.shard_map(
        on_device, mesh=mesh, in_specs=in_specs, out_specs=out_specs, check_vma=False
    )
```

time: 35 us -> 31.6 us (0.903)
  Pallas kernels: 31.6 us -> 29.6 us
  local copies, waits for them, and re-layouts: 2.53 us -> 1.18 us
    pallas_call x1, Pallas kernels: 31.6 us -> 29.6 us  [on_device(): pl.pallas_call(functools.partial(step_kernel, grps, tiles), out_shape=(pl...]
    unnamed x2, local copies, waits for them, and re-layouts: 2.53 us -> 1.18 us
where the time goes in v2:
time: 31.6 us; the launch traced here: 31.5 us
  Pallas kernels  29.6 us (94%)
  local copies, waits for them, and re-layouts  1.18 us (4%)
  between operations  0.64 us (2%)
    pallas_call x1, Pallas kernels, on_device(): pl.pallas_call(functools.partial(step_kernel, grps, tiles), out_shape=(pl...  29.6 us
    unnamed x2, local copies, waits for them, and re-layouts  1.18 us

profile of v2, /device:TPU:0, one launch (start us, length us, event | category | flops | bytes accessed | tf_op | source)
XLA Modules:
  0.0 31.5 jit_solution(146715340517331002)
XLA Ops:
  0.6 29.6 %shard_map.113 = (f32[2,256]{1,0:T(2,128)S(1)}, f32[14,128]{1,0:T(8,128)S(1)}) custom-call(bf16[3,1024,256]{2,1,0:T(8,128)(2,1)} %screens.1, bf16[12,256,256]{2,1,0:T(8,128)(2,1)} %bitcast.9, s32[3,4,256]{2,1,0:T(4,128)} %bitcast.10, f32[256,256]{1,0:T(8,128)} %illum.1, bf16[112,128,128]{2,1,0:T(8,128)(2,1)} %bitcast.8, s32[4,112]{1,0:T(4,128)} %bitcast.13, ...), custom_call_target="tpu_custom_call" | custom-call | tf_op jit(solution)/shard_map/pallas_call | solution.py:430
  30.3 0.6 %copy.14 = f32[2,256]{1,0:T(2,128)} copy(f32[2,256]{1,0:T(2,128)S(1)} %get-tuple-element.6) | data formatting | bytes 4096
  30.9 0.6 %copy.15 = f32[1792]{0:T(1024)} copy(f32[1792]{0:T(1024)S(1)} %bitcast.7) | data formatting | bytes 14336

commit v3 on v2

--- a/solution.py
+++ b/solution.py
@@ -51,6 +51,12 @@
 def one_hot(column, base, width):
     ids = lax.broadcasted_iota(jnp.int32, (column.shape[0], width), 1)
     return jnp.where(column - base == ids, 1.0, 0.0).astype(jnp.bfloat16)
+
+
+def ring(start, offset, size):
+    place = start + offset
+    place = jnp.where(place >= size, place - size, place)
+    return jnp.where(place >= size, place - size, place)
 
 
 def step_kernel(
@@ -83,6 +89,7 @@
     far_hot,
     wide_cm,
     words,
+    blocks,
     parts,
     sums,
     load_sem,
@@ -111,22 +118,13 @@
     my_tile = lax.axis_index("tile")
     me = my_grp * tiles + my_tile
     odd = lax.rem(me, 2)
-
-    def place(device):
-        return (device // tiles, device % tiles)
+    grp_peers = [ring(my_grp, offset, grps) for offset in range(grps)]
+    tile_peers = [ring(my_tile, offset, tiles) for offset in range(tiles)]
+    everyone = [(g, t) for t in tile_peers for g in grp_peers][1:]
 
     barrier = pltpu.get_barrier_semaphore()
-
-    def greet(offset, carry):
-        pl.semaphore_signal(
-            barrier,
-            inc=1,
-            device_id=place(lax.rem(me + offset, devices)),
-            device_id_type=MESH,
-        )
-        return carry
-
-    lax.fori_loop(1, devices, greet, 0)
+    for peer in everyone:
+        pl.semaphore_signal(barrier, inc=1, device_id=peer, device_id_type=MESH)
 
     loads = {}
     for number, (name, src, dst) in enumerate(
@@ -160,7 +158,9 @@
     far_copies, near_copies = [], []
     for kind, copies in enumerate((far_copies, near_copies)):
         ahead = odd if kind == 0 else 1 - odd
-        target = place(lax.rem(me + devices + 2 * ahead - 1, devices))
+        tile = my_tile + 2 * ahead - 1
+        turn = jnp.where(tile >= tiles, 1, jnp.where(tile < 0, -1, 0))
+        target = (ring(my_grp + turn, grps, grps), tile - turn * tiles)
         for layer in range(layers):
             copy = pltpu.make_async_remote_copy(
                 src_ref=screens.at[layer, pl.ds(pl.multiple_of(edge * ahead, reach), reach)],
@@ -258,25 +258,19 @@
     total = jnp.sum(intensity, axis=0, keepdims=True)
     slope_x = jnp.sum(intensity * centre_v, axis=0, keepdims=True) / total
     slope_y = jnp.sum(intensity * centre_u, axis=0, keepdims=True) / total
-    tile_row = lax.broadcasted_iota(jnp.int32, (SUBLANES, sub_dev), 0)
-    turned = jnp.where(
-        tile_row % 2 == 0,
-        jnp.broadcast_to(slope_x, tile_row.shape),
-        jnp.broadcast_to(slope_y, tile_row.shape),
-    )
-    turned = turned.astype(jnp.bfloat16).astype(jnp.float32)
-    for b in range(per_dev):
-        words[my_tile * per_dev + b] = turned[:, b * LANES : (b + 1) * LANES]
+    for c, slope in enumerate((slope_x, slope_y)):
+        for b in range(per_dev):
+            word = slope[:, b * LANES : (b + 1) * LANES].astype(jnp.bfloat16)
+            words[my_tile, pl.ds(c * per_dev + b, 1), :] = word.astype(jnp.float32)
 
     word_copies = []
-    mine = pl.ds(my_tile * per_dev, per_dev)
     for offset in range(1, tiles):
         copy = pltpu.make_async_remote_copy(
-            src_ref=words.at[mine],
-            dst_ref=words.at[mine],
+            src_ref=words.at[my_tile],
+            dst_ref=words.at[my_tile],
             send_sem=word_send.at[offset],
             recv_sem=word_recv.at[offset],
-            device_id=(my_grp, lax.rem(my_tile + offset, tiles)),
+            device_id=(my_grp, tile_peers[offset]),
             device_id_type=MESH,
         )
         copy.start()
@@ -285,6 +279,15 @@
     slopes_out[1:2, :] = slope_y
     for copy in word_copies:
         copy.wait_recv()
+
+    x_row = lax.broadcasted_iota(jnp.int32, (SUBLANES, LANES), 0) % 2 == 0
+    for d in range(tiles):
+        for b in range(per_dev):
+            blocks[d * per_dev + b] = jnp.where(
+                x_row,
+                jnp.broadcast_to(words[d, b : b + 1, :], x_row.shape),
+                jnp.broadcast_to(words[d, per_dev + b : per_dev + b + 1, :], x_row.shape),
+            )
 
     base_col = my_grp * (tiles * per_dev)
     act_row = (
@@ -298,7 +301,7 @@
             i = row * per_row + r
             products = jnp.zeros((tall, SUBLANES, LANES), jnp.float32)
             for n in range(nonzero):
-                block = words[jnp.maximum(cols_s[n, i] - base_col, 0)]
+                block = blocks[jnp.maximum(cols_s[n, i] - base_col, 0)]
                 products = products + wide_cm[i, n] * block[None]
             reduced = jnp.sum(products, axis=2, keepdims=True)
             spread = jnp.where(lane == r * acts + act_row, reduced, spread)
@@ -307,15 +310,15 @@
     partial = parts[my_grp]
 
     moved = first_grp * previous - gains * partial
-    lines = []
+    sum_lane = lax.broadcasted_iota(jnp.int32, sums.shape[1:], 1)
+    packed = jnp.zeros(sums.shape[1:], jnp.float32)
     for m in range(mirrors):
-        lines.append(jnp.sum(jnp.where(owners == m, moved, 0.0), axis=0, keepdims=True))
-    for m in range(mirrors):
-        lines.append(jnp.sum(jnp.where(owners == m, first_grp, 0.0), axis=0, keepdims=True))
-    sum_row = lax.broadcasted_iota(jnp.int32, sums.shape[1:], 0)
-    packed = jnp.zeros(sums.shape[1:], jnp.float32)
-    for number, line in enumerate(lines):
-        packed = jnp.where(sum_row == number, jnp.broadcast_to(line, packed.shape), packed)
+        amount = jnp.sum(jnp.where(owners == m, moved, 0.0), axis=0, keepdims=True)
+        number = jnp.sum(jnp.where(owners == m, first_grp, 0.0), axis=0, keepdims=True)
+        packed = jnp.where(sum_lane == m, jnp.sum(amount, axis=1, keepdims=True), packed)
+        packed = jnp.where(
+            sum_lane == mirrors + m, jnp.sum(number, axis=1, keepdims=True), packed
+        )
     sums[me] = packed
 
     part_copies = []
@@ -325,24 +328,21 @@
             dst_ref=parts.at[my_grp],
             send_sem=part_send.at[offset],
             recv_sem=part_recv.at[offset],
-            device_id=(lax.rem(my_grp + offset, grps), my_tile),
+            device_id=(grp_peers[offset], my_tile),
             device_id_type=MESH,
         )
         copy.start()
         part_copies.append(copy)
 
-    def send_sum(offset, carry):
+    for peer in everyone:
         pltpu.make_async_remote_copy(
             src_ref=sums.at[me],
             dst_ref=sums.at[me],
             send_sem=sum_send.at[0],
             recv_sem=sum_recv.at[0],
-            device_id=place(lax.rem(me + offset, devices)),
+            device_id=peer,
             device_id_type=MESH,
         ).start()
-        return carry
-
-    lax.fori_loop(1, devices, send_sum, 0)
     others = sums.at[pl.ds(0, devices - 1)]
     for copy in part_copies:
         copy.wait_recv()
@@ -351,16 +351,25 @@
         recon = recon + parts[g]
     updated = previous - gains * recon
     pltpu.make_async_copy(others, others, sum_recv.at[0]).wait()
-    everything = jnp.sum(jnp.sum(sums[...], axis=0), axis=1, keepdims=True)
+    everything = jnp.sum(sums[...], axis=0)
     piston = jnp.zeros(owners.shape, jnp.float32)
     for m in range(mirrors):
-        mean = everything[m : m + 1] / everything[mirrors + m : mirrors + m + 1]
+        mean = everything[:, m : m + 1] / everything[:, mirrors + m : mirrors + m + 1]
         piston = jnp.where(owners == m, mean, piston)
     commands_out[...] = updated - piston
 
     for copy in far_copies + near_copies + word_copies + part_copies:
         copy.wait_send()
     pltpu.make_async_copy(others, others, sum_send.at[0]).wait()
+
+
+def write_out(slopes, commands, slopes_out, commands_out, sem):
+    first = pltpu.make_async_copy(slopes, slopes_out, sem.at[0])
+    second = pltpu.make_async_copy(commands, commands_out, sem.at[1])
+    first.start()
+    second.start()
+    first.wait()
+    second.wait()
 
 
 def on_device(
@@ -390,7 +399,6 @@
     if spare:
         prev_commands = jnp.pad(prev_commands, (0, spare))
         owner_map = jnp.pad(owner_map, (0, spare), constant_values=-1)
-    sum_rows = -(-2 * mirrors // SUBLANES) * SUBLANES
     operands = (
         screens,
         interp_weights.reshape(layers * foot, pixels, pixels),
@@ -413,9 +421,10 @@
         pltpu.VMEM((layers, foot, sub_dev, pixels), jnp.bfloat16),
         pltpu.VMEM((layers, foot, sub_dev, reach), jnp.bfloat16),
         pltpu.VMEM((rowblk, nonzero, acts * comps // SUBLANES, SUBLANES, cbs), jnp.float32),
+        pltpu.VMEM((tiles, comps * per_dev, cbs), jnp.float32),
         pltpu.VMEM((tiles * per_dev, SUBLANES, cbs), jnp.float32),
         pltpu.VMEM((grps, rows, LANES), jnp.float32),
-        pltpu.VMEM((devices, sum_rows, LANES), jnp.float32),
+        pltpu.VMEM((devices, 1, LANES), jnp.float32),
         pltpu.SemaphoreType.DMA((9,)),
         pltpu.SemaphoreType.DMA((layers,)),
         pltpu.SemaphoreType.DMA((layers, 2)),
@@ -443,6 +452,16 @@
             collective_id=0, has_side_effects=True, vmem_limit_bytes=56 * 1024 * 1024
         ),
     )(*operands)
+    slopes, commands = pl.pallas_call(
+        write_out,
+        out_shape=(
+            jax.ShapeDtypeStruct(slopes.shape, slopes.dtype),
+            jax.ShapeDtypeStruct(commands.shape, commands.dtype),
+        ),
+        in_specs=[pl.BlockSpec(memory_space=pltpu.VMEM)] * 2,
+        out_specs=(pl.BlockSpec(memory_space=pltpu.HBM), pl.BlockSpec(memory_space=pltpu.HBM)),
+        scratch_shapes=[pltpu.SemaphoreType.DMA((2,))],
+    )(slopes, commands)
     return (slopes, commands.reshape(-1)[:act_dev])
 
 

time: 31.6 us -> 31.8 us (level)
    pallas_call x0 -> x1, Pallas kernels: none -> 1.31 us  [on_device(): pl.pallas_call(write_out, out_shape=(jax.ShapeDtypeStruct(slopes.shape, s...]
    pallas_call x1, Pallas kernels: 29.6 us -> 28.6 us  [on_device(): pl.pallas_call(functools.partial(step_kernel, grps, tiles), out_shape=(pl...]
    unnamed x2 -> x4, local copies, waits for them, and re-layouts: 1.18 us -> 1.16 us
where the time goes in v3:
time: 31.8 us; the launch traced here: 31.7 us
  Pallas kernels  29.9 us (94%)
  local copies, waits for them, and re-layouts  1.16 us (4%)
  between operations  0.65 us (2%)
    pallas_call x1, Pallas kernels, on_device(): pl.pallas_call(functools.partial(step_kernel, grps, tiles), out_shape=(pl...  28.6 us
    pallas_call x1, Pallas kernels, on_device(): pl.pallas_call(write_out, out_shape=(jax.ShapeDtypeStruct(slopes.shape, s...  1.31 us
    unnamed x4, local copies, waits for them, and re-layouts  1.16 us

profile of v3, /device:TPU:0, one launch (start us, length us, event | category | flops | bytes accessed | tf_op | source)
XLA Modules:
  0.0 31.7 jit_solution(6304270565063176632)
XLA Ops:
  0.6 28.6 %shard_map.113 = (f32[2,256]{1,0:T(2,128)S(1)}, f32[14,128]{1,0:T(8,128)S(1)}) custom-call(bf16[3,1024,256]{2,1,0:T(8,128)(2,1)} %screens.1, bf16[12,256,256]{2,1,0:T(8,128)(2,1)} %bitcast.8, s32[3,4,256]{2,1,0:T(4,128)} %bitcast.9, f32[256,256]{1,0:T(8,128)} %illum.1, bf16[112,128,128]{2,1,0:T(8,128)(2,1)} %bitcast.7, s32[4,112]{1,0:T(4,128)} %bitcast.12, ...), custom_call_target="tpu_custom_call" | custom-call | tf_op jit(solution)/shard_map/pallas_call | solution.py:439
  29.2 0.0 copy-start
  29.2 0.6 %copy-done = f32[14,128]{1,0:T(8,128)} copy-done((f32[14,128]{1,0:T(8,128)}, f32[14,128]{1,0:T(8,128)S(1)}, u32[]{:S(2)}) %copy-start) | copy-done | bytes 7192
  29.8 0.0 copy-start.1
  29.8 0.6 %copy-done.1 = f32[2,256]{1,0:T(2,128)} copy-done((f32[2,256]{1,0:T(2,128)}, f32[2,256]{1,0:T(2,128)S(1)}, u32[]{:S(2)}) %copy-start.1) | copy-done | bytes 2072
  30.4 1.3 %shard_map.114 = (f32[2,256]{1,0:T(2,128)}, f32[14,128]{1,0:T(8,128)}) custom-call(f32[2,256]{1,0:T(2,128)} %copy-done.1, f32[14,128]{1,0:T(8,128)} %copy-done), custom_call_target="tpu_custom_call" | custom-call | tf_op jit(solution)/shard_map/pallas_call | solution.py:455
Async XLA Ops:
  29.2 0.6 %copy-start = (f32[14,128]{1,0:T(8,128)}, f32[14,128]{1,0:T(8,128)S(1)}, u32[]{:S(2)}) copy-start(f32[14,128]{1,0:T(8,128)S(1)} %get-tuple-element.7.commands) | copy-start | bytes 21508
  29.8 0.6 %copy-start.1 = (f32[2,256]{1,0:T(2,128)}, f32[2,256]{1,0:T(2,128)S(1)}, u32[]{:S(2)}) copy-start(f32[2,256]{1,0:T(2,128)S(1)} %get-tuple-element.6.slopes) | copy-start | bytes 6148

commit v4 on v3

--- a/solution.py
+++ b/solution.py
@@ -48,9 +48,10 @@
     return cosine, sine
 
 
-def one_hot(column, base, width):
-    ids = lax.broadcasted_iota(jnp.int32, (column.shape[0], width), 1)
-    return jnp.where(column - base == ids, 1.0, 0.0).astype(jnp.bfloat16)
+def one_hot(ids, base, width):
+    lane = lax.broadcasted_iota(jnp.int32, ids.shape, 1) + base
+    hot = [jnp.where(ids == lane + first, 1.0, 0.0) for first in range(0, width, LANES)]
+    return jnp.concatenate(hot, 1).astype(jnp.bfloat16)
 
 
 def ring(start, offset, size):
@@ -85,6 +86,7 @@
     table_v,
     cols_s,
     gain_s,
+    ids_v,
     picked,
     far_hot,
     wide_cm,
@@ -174,23 +176,38 @@
             copies.append(copy)
 
     loads["foot"].wait()
-    columns = []
     for layer in range(layers):
         local = foot_v[layer] - (me * blk_dev - reach)
         local = jnp.where(local < 0, local + blk_dev * devices, local)
         local = jnp.where(local >= blk_dev * devices, local - blk_dev * devices, local)
         flipped = jnp.transpose(local)
-        columns.append([flipped[:, k : k + 1] for k in range(foot)])
+        for k in range(foot):
+            ids_v[layer, k * sub_dev : (k + 1) * sub_dev, :] = jnp.broadcast_to(
+                flipped[:, k : k + 1], (sub_dev, LANES)
+            )
+
+    def pick(layer, base, blocks_ref):
+        hot = one_hot(ids_v[layer], base, blocks_ref.shape[0])
+        return jnp.dot(hot, blocks_ref[...], preferred_element_type=jnp.float32).astype(
+            jnp.bfloat16
+        )
+
+    def weigh(layer, found):
+        side_by_side = jnp.concatenate(
+            [found[k * sub_dev : (k + 1) * sub_dev] for k in range(foot)], 1
+        )
+        own_weights = weights_v[layer * foot : (layer + 1) * foot]
+        return jnp.dot(
+            side_by_side,
+            own_weights.reshape(foot * pixels, pixels),
+            preferred_element_type=jnp.float32,
+        )
 
     for layer in range(layers):
         screen_loads[layer].wait()
-        for k in range(foot):
-            mine = jnp.dot(
-                one_hot(columns[layer][k], reach, blk_dev),
-                screens_v[layer],
-                preferred_element_type=jnp.float32,
-            )
-            picked[layer, k] = mine.astype(jnp.bfloat16)
+        picked[layer] = pick(layer, reach, screens_v.at[layer, pl.ds(0, reach)])
+        for first in range(reach, blk_dev, reach):
+            picked[layer] += pick(layer, reach + first, screens_v.at[layer, pl.ds(first, reach)])
 
     past = reach + blk_dev
     far_base, near_base = odd * past, (1 - odd) * past
@@ -198,26 +215,9 @@
     phase = jnp.zeros((sub_dev, pixels), jnp.float32)
     for layer in range(layers):
         near_copies[layer].wait_recv()
-        for k in range(foot):
-            column = columns[layer][k]
-            near = jnp.dot(
-                one_hot(column, near_base, reach),
-                halo[layer, 1],
-                preferred_element_type=jnp.float32,
-            )
-            both = picked[layer, k] + near.astype(jnp.bfloat16)
-            phase += jnp.dot(
-                both, weights_v[layer * foot + k], preferred_element_type=jnp.float32
-            )
-            far_hot[layer, k] = one_hot(column, far_base, reach)
-
-    loads["cm"].wait()
-
-    def widen(i, carry):
-        wide_cm[i] = cm_v[i].astype(jnp.float32).reshape(wide_cm.shape[1:])
-        return carry
-
-    lax.fori_loop(0, rowblk, widen, 0)
+        phase += weigh(layer, picked[layer] + pick(layer, near_base, halo.at[layer, 1]))
+    for layer in range(layers):
+        far_hot[layer] = one_hot(ids_v[layer], far_base, reach)
 
     for name in ("cols", "gain", "owner", "prev", "illum", "table"):
         loads[name].wait()
@@ -230,17 +230,8 @@
 
     for layer in range(layers):
         far_copies[layer].wait_recv()
-        other = jnp.dot(
-            far_hot[layer].reshape(foot * sub_dev, reach),
-            halo[layer, 0],
-            preferred_element_type=jnp.float32,
-        ).astype(jnp.bfloat16)
-        for k in range(foot):
-            phase += jnp.dot(
-                other[k * sub_dev : (k + 1) * sub_dev],
-                weights_v[layer * foot + k],
-                preferred_element_type=jnp.float32,
-            )
+        other = jnp.dot(far_hot[layer], halo[layer, 0], preferred_element_type=jnp.float32)
+        phase += weigh(layer, other.astype(jnp.bfloat16))
 
     cosine, sine = cos_sin(phase)
     bright = illum_v[...]
@@ -250,14 +241,21 @@
     )
     real_part, imag_part = spectrum[:pixels], spectrum[pixels:]
     intensity = real_part * real_part + imag_part * imag_part
-    freq = lax.broadcasted_iota(jnp.int32, (pixels, sub_dev), 0)
     half = SIDE // 2
-    freq_v, freq_u = freq % SIDE, freq // SIDE
-    centre_v = (freq_v - jnp.where(freq_v >= half, SIDE, 0)).astype(jnp.float32)
-    centre_u = (freq_u - jnp.where(freq_u >= half, SIDE, 0)).astype(jnp.float32)
-    total = jnp.sum(intensity, axis=0, keepdims=True)
-    slope_x = jnp.sum(intensity * centre_v, axis=0, keepdims=True) / total
-    slope_y = jnp.sum(intensity * centre_u, axis=0, keepdims=True) / total
+    wave = lax.broadcasted_iota(jnp.int32, (half, sub_dev), 0).astype(jnp.float32)
+    low_v = jnp.zeros((half, sub_dev), jnp.float32)
+    high_v = jnp.zeros((half, sub_dev), jnp.float32)
+    moment_u = jnp.zeros((half, sub_dev), jnp.float32)
+    for u in range(SIDE):
+        low = intensity[u * SIDE : u * SIDE + half]
+        high = intensity[u * SIDE + half : (u + 1) * SIDE]
+        low_v, high_v = low_v + low, high_v + high
+        centre_u = float(u - SIDE * (u >= half))
+        moment_u = moment_u + centre_u * (low + high)
+    moment_v = wave * low_v + (wave - half) * high_v
+    total = jnp.sum(low_v + high_v, axis=0, keepdims=True)
+    slope_x = jnp.sum(moment_v, axis=0, keepdims=True) / total
+    slope_y = jnp.sum(moment_u, axis=0, keepdims=True) / total
     for c, slope in enumerate((slope_x, slope_y)):
         for b in range(per_dev):
             word = slope[:, b * LANES : (b + 1) * LANES].astype(jnp.bfloat16)
@@ -277,6 +275,9 @@
         word_copies.append(copy)
     slopes_out[0:1, :] = slope_x
     slopes_out[1:2, :] = slope_y
+    loads["cm"].wait()
+    for i in range(rowblk):
+        wide_cm[i] = cm_v[i].astype(jnp.float32).reshape(wide_cm.shape[1:])
     for copy in word_copies:
         copy.wait_recv()
 
@@ -361,15 +362,6 @@
     for copy in far_copies + near_copies + word_copies + part_copies:
         copy.wait_send()
     pltpu.make_async_copy(others, others, sum_send.at[0]).wait()
-
-
-def write_out(slopes, commands, slopes_out, commands_out, sem):
-    first = pltpu.make_async_copy(slopes, slopes_out, sem.at[0])
-    second = pltpu.make_async_copy(commands, commands_out, sem.at[1])
-    first.start()
-    second.start()
-    first.wait()
-    second.wait()
 
 
 def on_device(
@@ -418,8 +410,9 @@
     for position in (5, 8):
         scratch.append(pltpu.SMEM(operands[position].shape, operands[position].dtype))
     scratch += [
-        pltpu.VMEM((layers, foot, sub_dev, pixels), jnp.bfloat16),
-        pltpu.VMEM((layers, foot, sub_dev, reach), jnp.bfloat16),
+        pltpu.VMEM((layers, foot * sub_dev, LANES), jnp.int32),
+        pltpu.VMEM((layers, foot * sub_dev, pixels), jnp.bfloat16),
+        pltpu.VMEM((layers, foot * sub_dev, reach), jnp.bfloat16),
         pltpu.VMEM((rowblk, nonzero, acts * comps // SUBLANES, SUBLANES, cbs), jnp.float32),
         pltpu.VMEM((tiles, comps * per_dev, cbs), jnp.float32),
         pltpu.VMEM((tiles * per_dev, SUBLANES, cbs), jnp.float32),
@@ -452,16 +445,6 @@
             collective_id=0, has_side_effects=True, vmem_limit_bytes=56 * 1024 * 1024
         ),
     )(*operands)
-    slopes, commands = pl.pallas_call(
-        write_out,
-        out_shape=(
-            jax.ShapeDtypeStruct(slopes.shape, slopes.dtype),
-            jax.ShapeDtypeStruct(commands.shape, commands.dtype),
-        ),
-        in_specs=[pl.BlockSpec(memory_space=pltpu.VMEM)] * 2,
-        out_specs=(pl.BlockSpec(memory_space=pltpu.HBM), pl.BlockSpec(memory_space=pltpu.HBM)),
-        scratch_shapes=[pltpu.SemaphoreType.DMA((2,))],
-    )(slopes, commands)
     return (slopes, commands.reshape(-1)[:act_dev])
 
 

time: 31.8 us -> 30.5 us (0.959)
  Pallas kernels: 29.9 us -> 28.5 us
    pallas_call x1 -> x0, Pallas kernels: 1.31 us -> none  [on_device(): pl.pallas_call(write_out, out_shape=(jax.ShapeDtypeStruct(slopes.shape, s...]
    unnamed x4 -> x2, local copies, waits for them, and re-layouts: 1.16 us -> 1.18 us
where the time goes in v4:
time: 30.5 us; the launch traced here: 30.4 us
  Pallas kernels  28.5 us (93%)
  local copies, waits for them, and re-layouts  1.18 us (4%)
  between operations  0.64 us (2%)
    pallas_call x1, Pallas kernels, on_device(): pl.pallas_call(functools.partial(step_kernel, grps, tiles), out_shape=(pl...  28.5 us
    unnamed x2, local copies, waits for them, and re-layouts  1.18 us

profile of v4, /device:TPU:0, one launch (start us, length us, event | category | flops | bytes accessed | tf_op | source)
XLA Modules:
  0.0 30.4 jit_solution(5344122510146578252)
XLA Ops:
  0.6 28.5 %shard_map.113 = (f32[2,256]{1,0:T(2,128)S(1)}, f32[14,128]{1,0:T(8,128)S(1)}) custom-call(bf16[3,1024,256]{2,1,0:T(8,128)(2,1)} %screens.1, bf16[12,256,256]{2,1,0:T(8,128)(2,1)} %bitcast.9, s32[3,4,256]{2,1,0:T(4,128)} %bitcast.10, f32[256,256]{1,0:T(8,128)} %illum.1, bf16[112,128,128]{2,1,0:T(8,128)(2,1)} %bitcast.8, s32[4,112]{1,0:T(4,128)} %bitcast.13, ...), custom_call_target="tpu_custom_call" | custom-call | tf_op jit(solution)/shard_map/pallas_call | solution.py:432
  29.2 0.6 %copy.14 = f32[2,256]{1,0:T(2,128)} copy(f32[2,256]{1,0:T(2,128)S(1)} %get-tuple-element.6) | data formatting | bytes 4096
  29.8 0.6 %copy.15 = f32[1792]{0:T(1024)} copy(f32[1792]{0:T(1024)S(1)} %bitcast.7) | data formatting | bytes 14336

commit v5 on v4

--- a/solution.py
+++ b/solution.py
@@ -12,6 +12,7 @@
 SIDE = 16
 LANES = 128
 SUBLANES = 8
+PIECES = 2
 MESH = pl.DeviceIdType.MESH
 
 
@@ -87,8 +88,11 @@
     cols_s,
     gain_s,
     ids_v,
+    asked,
+    asked_v,
+    answer_out,
+    answer_in,
     picked,
-    far_hot,
     wide_cm,
     words,
     blocks,
@@ -98,6 +102,10 @@
     screen_sem,
     halo_send,
     halo_recv,
+    ask_send,
+    ask_recv,
+    answer_send,
+    answer_recv,
     word_send,
     word_recv,
     part_send,
@@ -108,7 +116,7 @@
     layers, blk_dev, pixels = screens.shape
     foot = footprint.shape[1]
     sub_dev = illum.shape[0]
-    reach = halo.shape[2]
+    reach = halo.shape[1]
     mirrors = gain.shape[0]
     per_dev = sub_dev // LANES
     rowblk, nonzero, tall = wide_cm.shape[:3]
@@ -157,23 +165,34 @@
     pl.semaphore_wait(barrier, devices - 1)
 
     edge = blk_dev - reach
-    far_copies, near_copies = [], []
-    for kind, copies in enumerate((far_copies, near_copies)):
-        ahead = odd if kind == 0 else 1 - odd
-        tile = my_tile + 2 * ahead - 1
+
+    def beside(step):
+        tile = my_tile + step
         turn = jnp.where(tile >= tiles, 1, jnp.where(tile < 0, -1, 0))
-        target = (ring(my_grp + turn, grps, grps), tile - turn * tiles)
-        for layer in range(layers):
-            copy = pltpu.make_async_remote_copy(
-                src_ref=screens.at[layer, pl.ds(pl.multiple_of(edge * ahead, reach), reach)],
-                dst_ref=halo.at[layer, kind],
-                send_sem=halo_send.at[layer, kind],
-                recv_sem=halo_recv.at[layer, kind],
-                device_id=target,
-                device_id_type=MESH,
-            )
-            copy.start()
-            copies.append(copy)
+        return (ring(my_grp + turn, grps, grps), tile - turn * tiles)
+
+    far_place, near_place = beside(2 * odd - 1), beside(1 - 2 * odd)
+    ask = pltpu.make_async_remote_copy(
+        src_ref=footprint,
+        dst_ref=asked,
+        send_sem=ask_send.at[0],
+        recv_sem=ask_recv.at[0],
+        device_id=far_place,
+        device_id_type=MESH,
+    )
+    ask.start()
+    near_copies = []
+    for layer in range(layers):
+        copy = pltpu.make_async_remote_copy(
+            src_ref=screens.at[layer, pl.ds(pl.multiple_of(edge * (1 - odd), reach), reach)],
+            dst_ref=halo.at[layer],
+            send_sem=halo_send.at[layer],
+            recv_sem=halo_recv.at[layer],
+            device_id=near_place,
+            device_id_type=MESH,
+        )
+        copy.start()
+        near_copies.append(copy)
 
     loads["foot"].wait()
     for layer in range(layers):
@@ -186,15 +205,22 @@
                 flipped[:, k : k + 1], (sub_dev, LANES)
             )
 
-    def pick(layer, base, blocks_ref):
-        hot = one_hot(ids_v[layer], base, blocks_ref.shape[0])
+    def pick(ids, base, blocks_ref):
+        hot = one_hot(ids, base, blocks_ref.shape[0])
         return jnp.dot(hot, blocks_ref[...], preferred_element_type=jnp.float32).astype(
             jnp.bfloat16
         )
 
+    def pick_own(layer):
+        picked[layer] = pick(ids_v[layer], reach, screens_v.at[layer, pl.ds(0, reach)])
+        for first in range(reach, blk_dev, reach):
+            own = screens_v.at[layer, pl.ds(first, reach)]
+            picked[layer] += pick(ids_v[layer], reach + first, own)
+
     def weigh(layer, found):
+        count = found.shape[0] // foot
         side_by_side = jnp.concatenate(
-            [found[k * sub_dev : (k + 1) * sub_dev] for k in range(foot)], 1
+            [found[k * count : (k + 1) * count] for k in range(foot)], 1
         )
         own_weights = weights_v[layer * foot : (layer + 1) * foot]
         return jnp.dot(
@@ -203,21 +229,47 @@
             preferred_element_type=jnp.float32,
         )
 
+    screen_loads[0].wait()
+    pick_own(0)
+
+    ask.wait_recv()
+    pieces, piece = asked_v.shape[1], asked_v.shape[2] // foot
     for layer in range(layers):
+        flipped = jnp.transpose(asked[layer])
+        for k in range(foot):
+            for p in range(pieces):
+                asked_v[layer, p, k * piece : (k + 1) * piece, :] = jnp.broadcast_to(
+                    flipped[p * piece : (p + 1) * piece, k : k + 1], (piece, LANES)
+                )
+    first_edge = pl.multiple_of(edge * odd, reach)
+    loads["weights"].wait()
+    for layer in range(1, layers):
         screen_loads[layer].wait()
-        picked[layer] = pick(layer, reach, screens_v.at[layer, pl.ds(0, reach)])
-        for first in range(reach, blk_dev, reach):
-            picked[layer] += pick(layer, reach + first, screens_v.at[layer, pl.ds(first, reach)])
-
-    past = reach + blk_dev
-    far_base, near_base = odd * past, (1 - odd) * past
-    loads["weights"].wait()
+    answers = []
+    for p in range(pieces):
+        share = jnp.zeros((piece, pixels), jnp.float32)
+        for layer in range(layers):
+            at_edge = screens_v.at[layer, pl.ds(first_edge, reach)]
+            share += weigh(layer, pick(asked_v[layer, p], me * blk_dev + first_edge, at_edge))
+        answer_out[p] = share
+        answer = pltpu.make_async_remote_copy(
+            src_ref=answer_out.at[p],
+            dst_ref=answer_in.at[p],
+            send_sem=answer_send.at[p],
+            recv_sem=answer_recv.at[p],
+            device_id=far_place,
+            device_id_type=MESH,
+        )
+        answer.start()
+        answers.append(answer)
+
+    for layer in range(1, layers):
+        pick_own(layer)
+    near_base = (1 - odd) * (reach + blk_dev)
     phase = jnp.zeros((sub_dev, pixels), jnp.float32)
     for layer in range(layers):
         near_copies[layer].wait_recv()
-        phase += weigh(layer, picked[layer] + pick(layer, near_base, halo.at[layer, 1]))
-    for layer in range(layers):
-        far_hot[layer] = one_hot(ids_v[layer], far_base, reach)
+        phase += weigh(layer, picked[layer] + pick(ids_v[layer], near_base, halo.at[layer]))
 
     for name in ("cols", "gain", "owner", "prev", "illum", "table"):
         loads[name].wait()
@@ -228,11 +280,9 @@
         gains = jnp.where(owners == m, gain_s[m], gains)
     first_grp = jnp.where(my_grp == 0, 1.0, 0.0).astype(jnp.float32)
 
-    for layer in range(layers):
-        far_copies[layer].wait_recv()
-        other = jnp.dot(far_hot[layer], halo[layer, 0], preferred_element_type=jnp.float32)
-        phase += weigh(layer, other.astype(jnp.bfloat16))
-
+    for answer in answers:
+        answer.wait_recv()
+    phase += answer_in[...].reshape(sub_dev, pixels)
     cosine, sine = cos_sin(phase)
     bright = illum_v[...]
     field = jnp.concatenate([bright * cosine, bright * sine], 1).astype(jnp.bfloat16)
@@ -359,7 +409,7 @@
         piston = jnp.where(owners == m, mean, piston)
     commands_out[...] = updated - piston
 
-    for copy in far_copies + near_copies + word_copies + part_copies:
+    for copy in [ask] + answers + near_copies + word_copies + part_copies:
         copy.wait_send()
     pltpu.make_async_copy(others, others, sum_send.at[0]).wait()
 
@@ -404,15 +454,18 @@
         transform_table(SIDE),
     )
     scratch = [pltpu.VMEM(screens.shape, screens.dtype)]
-    scratch.append(pltpu.VMEM((layers, 2, reach, pixels), screens.dtype))
+    scratch.append(pltpu.VMEM((layers, reach, pixels), screens.dtype))
     for position in (1, 2, 3, 4, 6, 7, 9):
         scratch.append(pltpu.VMEM(operands[position].shape, operands[position].dtype))
     for position in (5, 8):
         scratch.append(pltpu.SMEM(operands[position].shape, operands[position].dtype))
     scratch += [
         pltpu.VMEM((layers, foot * sub_dev, LANES), jnp.int32),
+        pltpu.VMEM((layers, foot, sub_dev), jnp.int32),
+        pltpu.VMEM((layers, PIECES, foot * sub_dev // PIECES, LANES), jnp.int32),
+        pltpu.VMEM((PIECES, sub_dev // PIECES, pixels), jnp.float32),
+        pltpu.VMEM((PIECES, sub_dev // PIECES, pixels), jnp.float32),
         pltpu.VMEM((layers, foot * sub_dev, pixels), jnp.bfloat16),
-        pltpu.VMEM((layers, foot * sub_dev, reach), jnp.bfloat16),
         pltpu.VMEM((rowblk, nonzero, acts * comps // SUBLANES, SUBLANES, cbs), jnp.float32),
         pltpu.VMEM((tiles, comps * per_dev, cbs), jnp.float32),
         pltpu.VMEM((tiles * per_dev, SUBLANES, cbs), jnp.float32),
@@ -420,8 +473,12 @@
         pltpu.VMEM((devices, 1, LANES), jnp.float32),
         pltpu.SemaphoreType.DMA((9,)),
         pltpu.SemaphoreType.DMA((layers,)),
-        pltpu.SemaphoreType.DMA((layers, 2)),
-        pltpu.SemaphoreType.DMA((layers, 2)),
+        pltpu.SemaphoreType.DMA((layers,)),
+        pltpu.SemaphoreType.DMA((layers,)),
+        pltpu.SemaphoreType.DMA((1,)),
+        pltpu.SemaphoreType.DMA((1,)),
+        pltpu.SemaphoreType.DMA((PIECES,)),
+        pltpu.SemaphoreType.DMA((PIECES,)),
         pltpu.SemaphoreType.DMA((tiles,)),
         pltpu.SemaphoreType.DMA((tiles,)),
         pltpu.SemaphoreType.DMA((grps,)),

time: 30.5 us -> 31.9 us (1.046)
  Pallas kernels: 28.5 us -> 30 us
    pallas_call x1, Pallas kernels: 28.5 us -> 30 us  [on_device(): pl.pallas_call(functools.partial(step_kernel, grps, tiles), out_shape=(pl...]
where the time goes in v5:
time: 31.9 us; the launch traced here: 31.8 us
  Pallas kernels  30 us (94%)
  local copies, waits for them, and re-layouts  1.18 us (4%)
  between operations  0.64 us (2%)
    pallas_call x1, Pallas kernels, on_device(): pl.pallas_call(functools.partial(step_kernel, grps, tiles), out_shape=(pl...  30 us
    unnamed x2, local copies, waits for them, and re-layouts  1.18 us

profile of v5, /device:TPU:0, one launch (start us, length us, event | category | flops | bytes accessed | tf_op | source)
XLA Modules:
  0.0 31.8 jit_solution(17625640495894672504)
XLA Ops:
  0.6 30.0 %shard_map.113 = (f32[2,256]{1,0:T(2,128)S(1)}, f32[14,128]{1,0:T(8,128)S(1)}) custom-call(bf16[3,1024,256]{2,1,0:T(8,128)(2,1)} %screens.1, bf16[12,256,256]{2,1,0:T(8,128)(2,1)} %bitcast.9, s32[3,4,256]{2,1,0:T(4,128)} %bitcast.10, f32[256,256]{1,0:T(8,128)} %illum.1, bf16[112,128,128]{2,1,0:T(8,128)(2,1)} %bitcast.8, s32[4,112]{1,0:T(4,128)} %bitcast.13, ...), custom_call_target="tpu_custom_call" | custom-call | tf_op jit(solution)/shard_map/pallas_call | solution.py:489
  30.6 0.6 %copy.14 = f32[2,256]{1,0:T(2,128)} copy(f32[2,256]{1,0:T(2,128)S(1)} %get-tuple-element.6) | data formatting | bytes 4096
  31.2 0.6 %copy.15 = f32[1792]{0:T(1024)} copy(f32[1792]{0:T(1024)S(1)} %bitcast.7) | data formatting | bytes 14336

commit v6 on v4

--- a/solution.py
+++ b/solution.py
@@ -89,6 +89,7 @@
     ids_v,
     picked,
     far_hot,
+    both_cm,
     wide_cm,
     words,
     blocks,
@@ -111,8 +112,8 @@
     reach = halo.shape[2]
     mirrors = gain.shape[0]
     per_dev = sub_dev // LANES
-    rowblk, nonzero, tall = wide_cm.shape[:3]
-    acts = tall * SUBLANES // 2
+    rowblk, _, nonzero, tall = wide_cm.shape[:4]
+    acts = tall * SUBLANES
     rows = prev.shape[0]
     per_row = LANES // acts
     devices = grps * tiles
@@ -122,7 +123,9 @@
     odd = lax.rem(me, 2)
     grp_peers = [ring(my_grp, offset, grps) for offset in range(grps)]
     tile_peers = [ring(my_tile, offset, tiles) for offset in range(tiles)]
-    everyone = [(g, t) for t in tile_peers for g in grp_peers][1:]
+    steps = [(a, b) for b in range(tiles) for a in range(grps)][1:]
+    steps.sort(key=lambda step: (min(step[1], tiles - step[1]) != 1, step[0]))
+    everyone = [(grp_peers[a], tile_peers[b]) for a, b in steps]
 
     barrier = pltpu.get_barrier_semaphore()
     for peer in everyone:
@@ -219,6 +222,14 @@
     for layer in range(layers):
         far_hot[layer] = one_hot(ids_v[layer], far_base, reach)
 
+    loads["cm"].wait()
+    for i in range(rowblk):
+        both_cm[i] = cm_v[i].astype(jnp.float32)
+    for i in range(rowblk):
+        for c in range(2):
+            own = both_cm[i, pl.ds(c, nonzero * acts, stride=2), :]
+            wide_cm[i, c] = own.reshape(wide_cm.shape[2:])
+
     for name in ("cols", "gain", "owner", "prev", "illum", "table"):
         loads[name].wait()
     owners = owner_v[...]
@@ -275,26 +286,20 @@
         word_copies.append(copy)
     slopes_out[0:1, :] = slope_x
     slopes_out[1:2, :] = slope_y
-    loads["cm"].wait()
-    for i in range(rowblk):
-        wide_cm[i] = cm_v[i].astype(jnp.float32).reshape(wide_cm.shape[1:])
     for copy in word_copies:
         copy.wait_recv()
 
-    x_row = lax.broadcasted_iota(jnp.int32, (SUBLANES, LANES), 0) % 2 == 0
     for d in range(tiles):
         for b in range(per_dev):
-            blocks[d * per_dev + b] = jnp.where(
-                x_row,
-                jnp.broadcast_to(words[d, b : b + 1, :], x_row.shape),
-                jnp.broadcast_to(words[d, per_dev + b : per_dev + b + 1, :], x_row.shape),
-            )
+            for c in range(2):
+                row = words[d, c * per_dev + b : c * per_dev + b + 1, :]
+                blocks[d * per_dev + b, c] = jnp.broadcast_to(row, (SUBLANES, LANES))
 
     base_col = my_grp * (tiles * per_dev)
     act_row = (
         lax.broadcasted_iota(jnp.int32, (tall, SUBLANES, LANES), 0) * SUBLANES
         + lax.broadcasted_iota(jnp.int32, (tall, SUBLANES, LANES), 1)
-    ) // 2
+    )
     lane = lax.broadcasted_iota(jnp.int32, (tall, SUBLANES, LANES), 2)
     for row in range(rows):
         spread = jnp.zeros((tall, SUBLANES, LANES), jnp.float32)
@@ -303,7 +308,8 @@
             products = jnp.zeros((tall, SUBLANES, LANES), jnp.float32)
             for n in range(nonzero):
                 block = blocks[jnp.maximum(cols_s[n, i] - base_col, 0)]
-                products = products + wide_cm[i, n] * block[None]
+                for c in range(2):
+                    products = products + wide_cm[i, c, n] * block[c][None]
             reduced = jnp.sum(products, axis=2, keepdims=True)
             spread = jnp.where(lane == r * acts + act_row, reduced, spread)
         line = jnp.sum(jnp.sum(spread, axis=0), axis=0, keepdims=True)
@@ -362,6 +368,15 @@
     for copy in far_copies + near_copies + word_copies + part_copies:
         copy.wait_send()
     pltpu.make_async_copy(others, others, sum_send.at[0]).wait()
+
+
+def write_out(slopes, commands, slopes_out, commands_out, sem):
+    first = pltpu.make_async_copy(slopes, slopes_out, sem.at[0])
+    second = pltpu.make_async_copy(commands, commands_out, sem.at[1])
+    first.start()
+    second.start()
+    first.wait()
+    second.wait()
 
 
 def on_device(
@@ -413,9 +428,10 @@
         pltpu.VMEM((layers, foot * sub_dev, LANES), jnp.int32),
         pltpu.VMEM((layers, foot * sub_dev, pixels), jnp.bfloat16),
         pltpu.VMEM((layers, foot * sub_dev, reach), jnp.bfloat16),
-        pltpu.VMEM((rowblk, nonzero, acts * comps // SUBLANES, SUBLANES, cbs), jnp.float32),
+        pltpu.VMEM((rowblk, width, cbs), jnp.float32),
+        pltpu.VMEM((rowblk, comps, nonzero, acts // SUBLANES, SUBLANES, cbs), jnp.float32),
         pltpu.VMEM((tiles, comps * per_dev, cbs), jnp.float32),
-        pltpu.VMEM((tiles * per_dev, SUBLANES, cbs), jnp.float32),
+        pltpu.VMEM((tiles * per_dev, comps, SUBLANES, cbs), jnp.float32),
         pltpu.VMEM((grps, rows, LANES), jnp.float32),
         pltpu.VMEM((devices, 1, LANES), jnp.float32),
         pltpu.SemaphoreType.DMA((9,)),
@@ -445,6 +461,19 @@
             collective_id=0, has_side_effects=True, vmem_limit_bytes=56 * 1024 * 1024
         ),
     )(*operands)
+    slopes, commands = pl.pallas_call(
+        write_out,
+        out_shape=(
+            jax.ShapeDtypeStruct(slopes.shape, slopes.dtype),
+            jax.ShapeDtypeStruct(commands.shape, commands.dtype),
+        ),
+        in_specs=[pl.BlockSpec(memory_space=pltpu.VMEM)] * 2,
+        out_specs=(pl.BlockSpec(memory_space=pltpu.HBM), pl.BlockSpec(memory_space=pltpu.HBM)),
+        scratch_shapes=[pltpu.SemaphoreType.DMA((2,))],
+    )(
+        pltpu.with_memory_space_constraint(slopes, pltpu.VMEM),
+        pltpu.with_memory_space_constraint(commands, pltpu.VMEM),
+    )
     return (slopes, commands.reshape(-1)[:act_dev])
 
 

time: 30.5 us -> 29.7 us (0.974)
  local copies, waits for them, and re-layouts: 1.18 us -> 0 us
  Pallas kernels: 28.5 us -> 28.9 us
    unnamed x2 -> x0, local copies, waits for them, and re-layouts: 1.18 us -> none
    pallas_call x0 -> x1, Pallas kernels: none -> 0.62 us  [on_device(): pl.pallas_call(write_out, out_shape=(jax.ShapeDtypeStruct(slopes.shape, s...]
where the time goes in v6:
time: 29.7 us; the launch traced here: 29.6 us
  Pallas kernels  28.9 us (97%)
  between operations  0.64 us (2%)
    pallas_call x1, Pallas kernels, on_device(): pl.pallas_call(functools.partial(step_kernel, grps, tiles), out_shape=(pl...  28.3 us
    pallas_call x1, Pallas kernels, on_device(): pl.pallas_call(write_out, out_shape=(jax.ShapeDtypeStruct(slopes.shape, s...  0.62 us

profile of v6, /device:TPU:0, one launch (start us, length us, event | category | flops | bytes accessed | tf_op | source)
XLA Modules:
  0.0 29.6 jit_solution(15054456426983796147)
XLA Ops:
  0.6 28.3 %shard_map.113 = (f32[2,256]{1,0:T(2,128)S(1)}, f32[14,128]{1,0:T(8,128)S(1)}) custom-call(bf16[3,1024,256]{2,1,0:T(8,128)(2,1)} %screens.1, bf16[12,256,256]{2,1,0:T(8,128)(2,1)} %bitcast.8, s32[3,4,256]{2,1,0:T(4,128)} %bitcast.9, f32[256,256]{1,0:T(8,128)} %illum.1, bf16[112,128,128]{2,1,0:T(8,128)(2,1)} %bitcast.7, s32[4,112]{1,0:T(4,128)} %bitcast.12, ...), custom_call_target="tpu_custom_call" | custom-call | tf_op jit(solution)/shard_map/pallas_call | solution.py:448
  29.0 0.6 %shard_map.114 = (f32[2,256]{1,0:T(2,128)}, f32[14,128]{1,0:T(8,128)}) custom-call(f32[2,256]{1,0:T(2,128)S(1)} %get-tuple-element.6.slopes, f32[14,128]{1,0:T(8,128)S(1)} %get-tuple-element.7.commands), custom_call_target="tpu_custom_call" | custom-call | tf_op jit(solution)/shard_map/pallas_call | solution.py:464

commit v7 on v6

--- a/solution.py
+++ b/solution.py
@@ -166,12 +166,14 @@
         tile = my_tile + 2 * ahead - 1
         turn = jnp.where(tile >= tiles, 1, jnp.where(tile < 0, -1, 0))
         target = (ring(my_grp + turn, grps, grps), tile - turn * tiles)
-        for layer in range(layers):
+        for piece in range(2 * layers):
+            layer, start = piece // 2, (piece % 2) * (reach // 2)
+            first = pl.multiple_of(edge * ahead + start, reach // 2)
             copy = pltpu.make_async_remote_copy(
-                src_ref=screens.at[layer, pl.ds(pl.multiple_of(edge * ahead, reach), reach)],
-                dst_ref=halo.at[layer, kind],
-                send_sem=halo_send.at[layer, kind],
-                recv_sem=halo_recv.at[layer, kind],
+                src_ref=screens.at[layer, pl.ds(first, reach // 2)],
+                dst_ref=halo.at[layer, kind, pl.ds(start, reach // 2)],
+                send_sem=halo_send.at[piece, kind],
+                recv_sem=halo_recv.at[piece, kind],
                 device_id=target,
                 device_id_type=MESH,
             )
@@ -217,7 +219,8 @@
     loads["weights"].wait()
     phase = jnp.zeros((sub_dev, pixels), jnp.float32)
     for layer in range(layers):
-        near_copies[layer].wait_recv()
+        near_copies[2 * layer].wait_recv()
+        near_copies[2 * layer + 1].wait_recv()
         phase += weigh(layer, picked[layer] + pick(layer, near_base, halo.at[layer, 1]))
     for layer in range(layers):
         far_hot[layer] = one_hot(ids_v[layer], far_base, reach)
@@ -240,7 +243,8 @@
     first_grp = jnp.where(my_grp == 0, 1.0, 0.0).astype(jnp.float32)
 
     for layer in range(layers):
-        far_copies[layer].wait_recv()
+        far_copies[2 * layer].wait_recv()
+        far_copies[2 * layer + 1].wait_recv()
         other = jnp.dot(far_hot[layer], halo[layer, 0], preferred_element_type=jnp.float32)
         phase += weigh(layer, other.astype(jnp.bfloat16))
 
@@ -341,7 +345,7 @@
         copy.start()
         part_copies.append(copy)
 
-    for peer in everyone:
+    for peer in everyone[::-1]:
         pltpu.make_async_remote_copy(
             src_ref=sums.at[me],
             dst_ref=sums.at[me],
@@ -436,8 +440,8 @@
         pltpu.VMEM((devices, 1, LANES), jnp.float32),
         pltpu.SemaphoreType.DMA((9,)),
         pltpu.SemaphoreType.DMA((layers,)),
-        pltpu.SemaphoreType.DMA((layers, 2)),
-        pltpu.SemaphoreType.DMA((layers, 2)),
+        pltpu.SemaphoreType.DMA((2 * layers, 2)),
+        pltpu.SemaphoreType.DMA((2 * layers, 2)),
         pltpu.SemaphoreType.DMA((tiles,)),
         pltpu.SemaphoreType.DMA((tiles,)),
         pltpu.SemaphoreType.DMA((grps,)),

time: 29.7 us -> 29.8 us (level)
  no operation moved by 1% of the time
where the time goes in v7:
time: 29.8 us; the launch traced here: 29.6 us
  Pallas kernels  29 us (97%)
  between operations  0.64 us (2%)
    pallas_call x1, Pallas kernels, on_device(): pl.pallas_call(functools.partial(step_kernel, grps, tiles), out_shape=(pl...  28.4 us
    pallas_call x1, Pallas kernels, on_device(): pl.pallas_call(write_out, out_shape=(jax.ShapeDtypeStruct(slopes.shape, s...  0.62 us

profile of v7, /device:TPU:0, one launch (start us, length us, event | category | flops | bytes accessed | tf_op | source)
XLA Modules:
  0.0 29.6 jit_solution(15070592960209462959)
XLA Ops:
  0.6 28.4 %shard_map.113 = (f32[2,256]{1,0:T(2,128)S(1)}, f32[14,128]{1,0:T(8,128)S(1)}) custom-call(bf16[3,1024,256]{2,1,0:T(8,128)(2,1)} %screens.1, bf16[12,256,256]{2,1,0:T(8,128)(2,1)} %bitcast.8, s32[3,4,256]{2,1,0:T(4,128)} %bitcast.9, f32[256,256]{1,0:T(8,128)} %illum.1, bf16[112,128,128]{2,1,0:T(8,128)(2,1)} %bitcast.7, s32[4,112]{1,0:T(4,128)} %bitcast.12, ...), custom_call_target="tpu_custom_call" | custom-call | tf_op jit(solution)/shard_map/pallas_call | solution.py:452
  29.0 0.6 %shard_map.114 = (f32[2,256]{1,0:T(2,128)}, f32[14,128]{1,0:T(8,128)}) custom-call(f32[2,256]{1,0:T(2,128)S(1)} %get-tuple-element.6.slopes, f32[14,128]{1,0:T(8,128)S(1)} %get-tuple-element.7.commands), custom_call_target="tpu_custom_call" | custom-call | tf_op jit(solution)/shard_map/pallas_call | solution.py:468
